TPU v7x, 128 devices: a whole 4x4x4 slice. The times are simulated.
128 devices in a mesh: rep: 4 (over z), exp: 32 (over y, x, core).
Axes of the slice: x: 4, y: 4, z: 4, core: 2. Of those that a mesh axis runs over, the one named last changes fastest.
Arguments:
- hidden_in: bfloat16 [32768, 768], P(('rep', 'exp')), may hold values from -6 to 6
- doc_ids: int32 [32768], P(('rep', 'exp')), may hold values from 0 to 127, as said below
- routes: int32 [32768, 1], P(('rep', 'exp')), may hold values from 0 to 31; in each aligned block of 256 rows (0 to 255, 256 to 511, ...) at most 16 rows name the same one
- attn_gain: bfloat16 [768], P('exp'), may hold values from 0.5 to 1.5
- w_query: bfloat16 [768, 768], P('exp'), may hold values from -0.21875 to 0.21875
- w_key: bfloat16 [768, 768], P('exp'), may hold values from -0.21875 to 0.21875
- w_value: bfloat16 [768, 768], P('exp'), may hold values from -0.21875 to 0.21875
- w_out: bfloat16 [768, 768], P('exp'), may hold values from -0.625 to 0.625
- rel_bias: bfloat16 [32, 12], P('exp'), may hold values from -4 to 4
- ffn_gain: bfloat16 [768], P('exp'), may hold values from 0.5 to 1.5
- w_router: bfloat16 [768, 32], P('exp'), may hold values from -0.109375 to 0.109375
- w_in: bfloat16 [32, 768, 3072], P('exp'), may hold values from -0.21875 to 0.21875
- w_down: bfloat16 [32, 3072, 768], P('exp'), may hold values from -6 to 6
- out_grad: bfloat16 [32768, 768], P(('rep', 'exp')), may hold values from -6 to 6
Outputs:
- block_out: bfloat16 [32768, 768], P(('rep', 'exp'))
- grad_in: float32 [32768, 768], P(('rep', 'exp'))
- grad_attn_gain: float32 [768], P('exp')
- grad_query: float32 [768, 768], P('exp')
- grad_key: float32 [768, 768], P('exp')
- grad_value: float32 [768, 768], P('exp')
- grad_out: float32 [768, 768], P('exp')
- grad_rel_bias: float32 [32, 12], P('exp')
- grad_ffn_gain: float32 [768], P('exp')
- grad_router: float32 [768, 32], P('exp')
- grad_w_in: float32 [32, 768, 3072], P('exp', None, 'rep')
- grad_w_down: float32 [32, 3072, 768], P('exp', 'rep')
Inputs may be any that keep to these rules, and one draw needn't show every extreme that they name: `doc_ids`: within each block of 256 consecutive tokens (one device's) the ids start at 0 and never fall; a sequence is a run of equal ids and starts at an even position of its block; the first block is a single sequence. `routes`: among the tokens of one device no expert is named more than 16 times.
All inputs are finite; a program needn't handle non-finite values.
Results may differ from a plain program's by a relative error of at most 0.028.
Values may be sent and summed in bfloat16 or wider, within the bound.
No kernel may reach another device: no remote copies, remote signals or barrier semaphores. Data moves between devices by JAX's collectives and lax.ppermute only.
A program may use at most 128 MiB of HBM per device.

v0:
```python
import jax
import jax.numpy as jnp
from jax import lax
from jax.experimental import pallas as pl
from jax.experimental.pallas import tpu as pltpu
from jax.sharding import PartitionSpec as P

HEADS = 12
HEAD_DIM = 64
BUCKETS = 32
D = 768
FF = 3072
TOK = 256
EXPERTS = 32
CAP = 16
SLOTS = EXPERTS * CAP
HALF = D // 2
QKV = 3 * HALF
WIDE1 = QKV + 128
WIDE2 = D + 128
WIDE = D + 128
SENT = QKV + HALF + 128
AT_FFN = EXPERTS
AT_ATTN = EXPERTS + 1
AT_BIAS = EXPERTS + 2

eps = 1e-06
reach_marks = (12, 16, 23, 32, 46, 64, 91)
big_negative = -1000000000.0
score_scale = HEAD_DIM ** (-0.5)

f32 = jnp.float32
bf16 = jnp.bfloat16
HIGHEST = lax.Precision.HIGHEST

NN = ((1,), (0,))
NT = ((1,), (1,))
TN = ((0,), (0,))

SWAP = [(i, i ^ 1) for i in range(32)]


def z_shift(step):
    return [(i, (i + step) % 4) for i in range(4)]


def on_exp(value, pairs):
    return lax.ppermute(value, "exp", pairs)


def dot(left, right, dims, precision=None):
    return lax.dot_general(
        left, right, (dims, ((), ())), precision=precision, preferred_element_type=f32
    )


def call(body, outs, *args, scratch=(), smem=1, after=(), flops=0, bytes_accessed=0):
    count = len(args)
    specs = [
        pl.BlockSpec(memory_space=pltpu.SMEM) if i < smem else pl.BlockSpec()
        for i in range(count)
    ]
    specs += [pl.BlockSpec(memory_space=pl.ANY) for _ in after]

    def run(*refs):
        body(*refs[:count], *refs[count + len(after) :])

    return pl.pallas_call(
        run,
        out_shape=[jax.ShapeDtypeStruct(shape, kind) for shape, kind in outs],
        in_specs=specs,
        out_specs=[pl.BlockSpec() for _ in outs],
        scratch_shapes=list(scratch),
        compiler_params=pltpu.CompilerParams(vmem_limit_bytes=60 * 1024 * 1024),
        cost_estimate=pl.CostEstimate(
            flops=flops, bytes_accessed=bytes_accessed, transcendentals=0
        ),
    )(*args, *after)


def pack_weights(query, key, value, out, router, attn_gain, ffn_gain, bias, packed, beside):
    same = lax.broadcasted_iota(jnp.int32, (24, 24), 0) == lax.broadcasted_iota(
        jnp.int32, (24, 24), 1
    )

    def column(row):
        spread = jnp.broadcast_to(row[...].astype(f32), (24, 24))
        return jnp.sum(jnp.where(same, spread, 0.0), axis=1, keepdims=True)

    first = lax.broadcasted_iota(jnp.int32, (24, HEADS), 0) == 0
    table = jnp.where(first, jnp.broadcast_to(bias[...].astype(f32), (24, HEADS)), 0.0)
    extra = jnp.concatenate(
        [
            router[...].astype(f32),
            column(ffn_gain),
            column(attn_gain),
            table,
            jnp.zeros((24, 128 - AT_BIAS - HEADS), f32),
        ],
        axis=1,
    ).astype(bf16)
    beside[:, :D] = out[...]
    beside[:, D:] = extra
    for core in range(2):
        columns = slice(core * HALF, (core + 1) * HALF)
        half = jnp.concatenate(
            [query[:, columns], key[:, columns], value[:, columns], extra], axis=1
        )
        for chip in range(16):
            packed[2 * chip + core] = half


def sum_parts(parts, own):
    for core in range(2):
        total = parts[core].astype(f32)
        for chip in range(1, 16):
            total = total + parts[2 * chip + core].astype(f32)
        own[:, core * SENT : (core + 1) * SENT] = total.astype(bf16)


def diagonal_buckets():
    lane = lax.broadcasted_iota(jnp.int32, (8, 512), 1)
    row = lax.broadcasted_iota(jnp.int32, (8, 512), 0)
    relative = lane - row - 255
    distance = jnp.abs(relative)
    far = jnp.full((8, 512), 8, jnp.int32)
    for mark in reach_marks:
        far = far + (distance >= mark).astype(jnp.int32)
    return jnp.where(distance < 8, distance, far) + jnp.where(relative > 0, 16, 0)


def bucket_hot(buckets, row):
    which = lax.broadcasted_iota(jnp.int32, (BUCKETS, 512), 0)
    return (which == jnp.broadcast_to(buckets[row : row + 1], (BUCKETS, 512))).astype(f32)


def owner_rows():
    row = lax.broadcasted_iota(jnp.int32, (BUCKETS, D), 0)
    column = lax.broadcasted_iota(jnp.int32, (BUCKETS, D), 1)
    return (column == row * 24).astype(bf16)


def gain_row(extra, lane):
    pick = (lax.broadcasted_iota(jnp.int32, (8, 128), 1) == lane).astype(bf16)
    return dot(pick, extra, NT)[0:1]


def inverse_rms(values):
    return lax.rsqrt(jnp.mean(values * values, axis=-1, keepdims=True) + eps)


def attention_forward(pos, x_own, x_other, doc_col, doc_row, weights, *refs):
    attn_in, projected, probs, attended_own, attended_other, base = refs
    extra = weights[:, QKV:]
    gain = gain_row(extra, AT_ATTN)
    head = lax.broadcasted_iota(jnp.int32, (128, 16), 1)
    moved = (lax.broadcasted_iota(jnp.int32, (128, 16), 0) == head + AT_BIAS).astype(bf16)
    table = dot(dot(extra, moved, NN).astype(bf16), owner_rows(), ((0,), (1,)))
    buckets = diagonal_buckets()
    for row in range(8):
        base[:, row, :] = dot(table.astype(bf16), bucket_hot(buckets, row).astype(bf16), NN)
    for block, x_ref in enumerate((x_own, x_other)):
        x = x_ref[...].astype(f32)
        attn_in[block * TOK : (block + 1) * TOK] = (x * inverse_rms(x) * gain).astype(bf16)
    for part in range(3):
        columns = slice(part * HALF, (part + 1) * HALF)
        projected[:, columns] = dot(attn_in[...], weights[:, columns], NN).astype(bf16)
    left = lax.broadcasted_iota(jnp.int32, (TOK, 128), 1) < 64
    first_head = pos[2] * (HEADS // 2)
    for block, attended in enumerate((attended_own, attended_other)):
        rows = slice(block * TOK, (block + 1) * TOK)
        same = doc_col[rows] == doc_row[block : block + 1]

        def pair_step(pair, carry):
            start = pair * 128
            queries = projected[rows, pl.ds(pl.multiple_of(start, 128), 128)]
            keys = projected[rows, pl.ds(pl.multiple_of(start + HALF, 128), 128)]
            values = projected[rows, pl.ds(pl.multiple_of(start + 2 * HALF, 128), 128)]
            results = []
            for side in range(2):
                mine = left if side == 0 else jnp.logical_not(left)
                own = jnp.where(mine, queries, jnp.zeros_like(queries))
                diagonal = base[first_head + 2 * pair + side]
                bias = jnp.concatenate(
                    [pltpu.roll(diagonal, 257 + 8 * g, 1)[:, :256] for g in range(32)], axis=0
                )
                scores = jnp.where(same, score_scale * dot(own, keys, NT) + bias, big_negative)
                top = jnp.max(scores, axis=-1, keepdims=True)
                grown = jnp.exp(scores - top)
                share = grown * (1.0 / jnp.sum(grown, axis=-1, keepdims=True))
                share = share.astype(bf16)
                probs[block * (HEADS // 2) + 2 * pair + side] = share
                results.append(dot(share, values, NN))
            attended[:, pl.ds(pl.multiple_of(start, 128), 128)] = jnp.where(
                left, results[0], results[1]
            ).astype(bf16)
            return carry

        lax.fori_loop(0, HEADS // 4, pair_step, 0)


def in_parts(value, rows):
    lane = lax.broadcasted_iota(jnp.int32, (rows, 128), 1)
    high = value.astype(bf16).astype(f32)
    middle = (value - high).astype(bf16).astype(f32)
    low = value - high - middle
    parts = jnp.where(lane == 0, high, jnp.where(lane == 1, middle, jnp.where(lane == 2, low, 0.0)))
    return parts.astype(bf16)


def from_parts(parts):
    return jnp.sum(parts.astype(f32), axis=-1, keepdims=True)


def place_grads(routes, out_grad, placer, placed_grads):
    lane = lax.broadcasted_iota(jnp.int32, (TOK, 128), 1)
    chosen = routes[...] == lane
    earlier = (
        lax.broadcasted_iota(jnp.int32, (TOK, TOK), 1)
        < lax.broadcasted_iota(jnp.int32, (TOK, TOK), 0)
    ).astype(bf16)
    counts = dot(earlier, chosen.astype(bf16), NN)
    rank = jnp.sum(jnp.where(chosen, counts, 0.0), axis=-1, keepdims=True)
    slot = routes[...] * CAP + rank.astype(jnp.int32)
    placed = (slot == lax.broadcasted_iota(jnp.int32, (TOK, SLOTS), 1)).astype(bf16)
    placer[...] = placed
    placed_grads[...] = dot(placed, out_grad[...], TN).astype(bf16)


def hold(value, until, out):
    del value, until, out


def hold_until(value, until):
    return pl.pallas_call(
        hold,
        out_shape=jax.ShapeDtypeStruct(value.shape, value.dtype),
        in_specs=[pl.BlockSpec(memory_space=pl.ANY)] * 2,
        out_specs=pl.BlockSpec(memory_space=pl.ANY),
        input_output_aliases={0: 0},
    )(value, until)


def core_halves(pos):
    own = pl.ds(pl.multiple_of(pos[2] * HALF, 128), HALF)
    other = pl.ds(pl.multiple_of((1 - pos[2]) * HALF, 128), HALF)
    return own, other


def route_forward(pos, x_ref, routes, att_own, att_other, placer, weights, *refs):
    after, ffn_in, router, gate, outbound = refs
    own, other = core_halves(pos)
    extra = weights[:, D:]
    gain = gain_row(extra, AT_FFN)
    after_attn = (
        x_ref[...].astype(f32)
        + dot(att_own[...], weights[own, :D], NN)
        + dot(att_other[...], weights[other, :D], NN)
    )
    after[...] = after_attn
    ffn_input = (after_attn * inverse_rms(after_attn) * gain).astype(bf16)
    ffn_in[...] = ffn_input
    lane = lax.broadcasted_iota(jnp.int32, (TOK, 128), 1)
    logits = dot(ffn_input, extra, NN)
    logits = jnp.where(lane < EXPERTS, logits, -1e30)
    grown = jnp.exp(logits - jnp.max(logits, axis=-1, keepdims=True))
    share = grown / jnp.sum(grown, axis=-1, keepdims=True)
    router[...] = share
    gates = jnp.sum(jnp.where(routes[...] == lane, share, 0.0), axis=-1, keepdims=True)
    gate[...] = gates
    outbound[:, :D] = dot(placer[...], ffn_input, TN).astype(bf16)
    outbound[:, D:] = dot(placer[...], in_parts(gates, TOK), TN).astype(bf16)


def gelu_parts(pre):
    square = pre * pre
    inner = 0.7978845608028654 * pre * (1.0 + 0.044715 * square)
    bend = jnp.tanh(inner)
    cdf = 0.5 * (1.0 + bend)
    slope = cdf + 0.5 * pre * (1.0 - bend * bend) * (
        0.7978845608028654 * (1.0 + 0.134145 * square)
    )
    return pre * cdf, slope


def expert_block(rows, mix, w_in, w_down, produced, back, total, back_total, grads):
    step = pl.program_id(0)

    @pl.when(step == 0)
    def _():
        grads[...] = (from_parts(rows[:, D:]) * mix[...].astype(f32)).astype(bf16)

    active, slope = gelu_parts(dot(rows[:, :D], w_in[0], NN))
    grad_pre = (dot(grads[...], w_down[0], NT) * slope).astype(bf16)
    forward = dot(active.astype(bf16), w_down[0], NN)
    backward = dot(grad_pre, w_in[0], NT)

    @pl.when(step == 0)
    def _():
        total[...] = forward
        back_total[...] = backward

    @pl.when(step > 0)
    def _():
        total[...] += forward
        back_total[...] += backward

    @pl.when(step == pl.num_programs(0) - 1)
    def _():
        out = total[...].astype(bf16)
        produced[...] = out
        back[:, :D] = back_total[...].astype(bf16)
        per_gate = jnp.sum(mix[...].astype(f32) * out.astype(f32), axis=-1, keepdims=True)
        back[:, D:] = in_parts(per_gate, SLOTS)


def expert_weights(pos, *refs):
    all_rows, all_mix, w_in, w_down, _, grad_in, grad_down = refs
    for k in range(4):
        group = slice(k * SLOTS, (k + 1) * SLOTS)
        own = all_rows[group, :D]
        grads = (from_parts(all_rows[group, D:]) * all_mix[group].astype(f32)).astype(bf16)
        active, slope = gelu_parts(dot(own, w_in[0], NN))
        grad_pre = (dot(grads, w_down[0], NT) * slope).astype(bf16)
        to_in = dot(own, grad_pre, TN)
        to_down = dot(active.astype(bf16), grads, TN)
        if k == 0:
            grad_in[0] = to_in
            grad_down[0] = to_down
        else:
            grad_in[0] += to_in
            grad_down[0] += to_down


BLOCK = 512
WBLOCK = 256


def run_expert(rows, mix, w_in, w_down):
    wide = pl.BlockSpec((SLOTS, WIDE), lambda f: (0, 0))
    whole = pl.BlockSpec((SLOTS, D), lambda f: (0, 0))
    return pl.pallas_call(
        expert_block,
        grid=(FF // BLOCK,),
        in_specs=[
            wide,
            whole,
            pl.BlockSpec((1, D, BLOCK), lambda f: (0, 0, f)),
            pl.BlockSpec((1, BLOCK, D), lambda f: (0, f, 0)),
        ],
        out_specs=[whole, wide],
        out_shape=[
            jax.ShapeDtypeStruct((SLOTS, D), bf16),
            jax.ShapeDtypeStruct((SLOTS, WIDE), bf16),
        ],
        scratch_shapes=[
            pltpu.VMEM((SLOTS, D), f32),
            pltpu.VMEM((SLOTS, D), f32),
            pltpu.VMEM((SLOTS, D), bf16),
        ],
        compiler_params=pltpu.CompilerParams(vmem_limit_bytes=60 * 1024 * 1024),
        cost_estimate=pl.CostEstimate(
            flops=8 * SLOTS * D * FF, bytes_accessed=14 * 1024 * 1024, transcendentals=0
        ),
    )(rows, mix, w_in, w_down)


def run_expert_weights(group, rows, mix, w_in, w_down, after):
    steps = D // WBLOCK
    return pl.pallas_call(
        expert_weights,
        grid_spec=pltpu.PrefetchScalarGridSpec(
            num_scalar_prefetch=1,
            grid=(steps,),
            in_specs=[
                pl.BlockSpec((4 * SLOTS, WIDE), lambda f, g: (0, 0)),
                pl.BlockSpec((4 * SLOTS, D), lambda f, g: (0, 0)),
                pl.BlockSpec((1, D, WBLOCK), lambda f, g: (0, 0, g[0] * steps + f)),
                pl.BlockSpec((1, WBLOCK, D), lambda f, g: (0, g[0] * steps + f, 0)),
                pl.BlockSpec(memory_space=pl.ANY),
            ],
            out_specs=[
                pl.BlockSpec((1, D, WBLOCK), lambda f, g: (0, 0, f)),
                pl.BlockSpec((1, WBLOCK, D), lambda f, g: (0, f, 0)),
            ],
        ),
        out_shape=[
            jax.ShapeDtypeStruct((1, D, D), f32),
            jax.ShapeDtypeStruct((1, D, D), f32),
        ],
        compiler_params=pltpu.CompilerParams(vmem_limit_bytes=60 * 1024 * 1024),
        cost_estimate=pl.CostEstimate(
            flops=32 * SLOTS * D * D, bytes_accessed=14 * 1024 * 1024, transcendentals=0
        ),
    )(group, rows, mix, w_in, w_down, after)


def mix_out(after, gate, placer, returned, block_out):
    expert_out = dot(placer[...], returned[...], NN)
    block_out[...] = (after[...] + gate[...] * expert_out).astype(bf16)


def norm_backward(values, grads, gain):
    inverse = inverse_rms(values)
    normed = values * inverse
    per_gain = grads * normed
    scaled = grads * gain
    back = inverse * (scaled - normed * jnp.mean(scaled * normed, axis=-1, keepdims=True))
    return back, per_gain


def column_sums(values):
    return dot(values, jnp.ones((values.shape[0], 128), f32), TN, HIGHEST)


def route_backward(pos, *refs):
    (routes, out_grad, att_own, att_other, after, ffn_in, router, gate, placer, grad_back, weights) = refs[:11]
    grad_after, grad_own, grad_other, keep, send, whole = refs[11:]
    extra_weights = weights[:, D:]
    gain = gain_row(extra_weights, AT_FFN)
    grad_mix = out_grad[...].astype(f32)
    after_attn = after[...]
    gates = gate[...]
    lane = lax.broadcasted_iota(jnp.int32, (TOK, 128), 1)
    grad_gate = from_parts(dot(placer[...], grad_back[:, D:], NN))
    chosen = (routes[...] == lane).astype(f32)
    grad_logits = (router[...] * (chosen - gates) * grad_gate).astype(bf16)
    router_weights = jnp.where(
        lax.broadcasted_iota(jnp.int32, (D, 128), 1) < EXPERTS, extra_weights, jnp.zeros((D, 128), bf16)
    )
    grad_ffn = dot(placer[...], grad_back[:, :D], NN) + dot(grad_logits, router_weights, NT)
    back, per_gain = norm_backward(after_attn, grad_ffn, gain)
    grad_after_attn = grad_mix + back
    grad_after[...] = grad_after_attn
    branch = grad_after_attn.astype(bf16)
    own, other = core_halves(pos)
    grad_own[...] = dot(branch, weights[own, :D], NT).astype(bf16)
    grad_other[...] = dot(branch, weights[other, :D], NT).astype(bf16)
    whole[own, :] = dot(att_own[...], branch, TN).astype(bf16)
    whole[other, :] = dot(att_other[...], branch, TN).astype(bf16)
    keep[:, :HALF] = whole[:, own]
    send[...] = whole[:, other]
    tall = lax.broadcasted_iota(jnp.int32, (D, 128), 1)
    extra = dot(ffn_in[...], grad_logits, TN)
    keep[:, HALF:] = jnp.where(tall == AT_FFN, column_sums(per_gain), extra).astype(bf16)


def attention_backward(pos, projected, probs, grad_own, grad_other, grad_projected, diagonals):
    left = lax.broadcasted_iota(jnp.int32, (TOK, 128), 1) < 64
    diagonals[...] = jnp.zeros_like(diagonals)
    first_head = pos[2] * (HEADS // 2)
    for block, grad_att in enumerate((grad_own, grad_other)):
        rows = slice(block * TOK, (block + 1) * TOK)

        def pair_step(pair, carry):
            start = pair * 128
            at_query = pl.ds(pl.multiple_of(start, 128), 128)
            at_key = pl.ds(pl.multiple_of(start + HALF, 128), 128)
            at_value = pl.ds(pl.multiple_of(start + 2 * HALF, 128), 128)
            queries, keys, values = (
                projected[rows, at_query],
                projected[rows, at_key],
                projected[rows, at_value],
            )
            grads = grad_att[:, at_query]
            to_query, to_key, to_value = [], [], []
            for side in range(2):
                mine = left if side == 0 else jnp.logical_not(left)
                own = jnp.where(mine, grads, jnp.zeros_like(grads))
                share16 = probs[block * (HEADS // 2) + 2 * pair + side]
                share = share16.astype(f32)
                grad_probs = dot(own, values, NT)
                to_value.append(dot(share16, grads, TN))
                mixed = share * grad_probs
                grad_scores = mixed - share * jnp.sum(mixed, axis=-1, keepdims=True)
                grad16 = grad_scores.astype(bf16)
                to_query.append(dot(grad16, keys, NN))
                to_key.append(dot(grad16, queries, TN))
                rounded = grad16.astype(f32)
                total = jnp.zeros((8, 512), f32)
                blank = jnp.zeros((8, 256), f32)
                for g in range(32):
                    lines = jnp.concatenate([rounded[8 * g : 8 * g + 8], blank], axis=1)
                    total = total + pltpu.roll(lines, 255 - 8 * g, 1)
                diagonals[first_head + 2 * pair + side] += total
            grad_projected[rows, at_query] = (score_scale * jnp.where(left, *to_query)).astype(bf16)
            grad_projected[rows, at_key] = (score_scale * jnp.where(left, *to_key)).astype(bf16)
            grad_projected[rows, at_value] = jnp.where(left, *to_value).astype(bf16)
            return carry

        lax.fori_loop(0, HEADS // 4, pair_step, 0)


def weights_backward(x_own, x_other, attn_in, grad_projected, weights, diagonals, keep, got, *refs):
    whole, to_own, to_other = refs
    whole[:, :QKV] = dot(attn_in[...], grad_projected[...], TN).astype(bf16)
    whole[:, QKV : QKV + HALF] = (keep[:, :HALF].astype(f32) + got[...].astype(f32)).astype(bf16)
    sums = jnp.zeros((D, 128), f32)
    for block, (x_ref, out) in enumerate(((x_own, to_own), (x_other, to_other))):
        rows = slice(block * TOK, (block + 1) * TOK)
        grads = dot(grad_projected[rows], weights[:, :QKV], NT)
        out[...] = grads
        x = x_ref[...].astype(f32)
        sums = sums + column_sums(grads * (x * inverse_rms(x)))
    buckets = diagonal_buckets()
    per_bucket = jnp.zeros((BUCKETS, 16), f32)
    for row in range(8):
        per_bucket = per_bucket + dot(bucket_hot(buckets, row), diagonals[:, row, :], NT, HIGHEST)
    head = lax.broadcasted_iota(jnp.int32, (16, 128), 0)
    moved = (lax.broadcasted_iota(jnp.int32, (16, 128), 1) == head + AT_BIAS).astype(bf16)
    per_bucket = dot(per_bucket.astype(bf16), moved, NN)
    tall = lax.broadcasted_iota(jnp.int32, (D, 128), 1)
    extra = keep[:, HALF:].astype(f32) + dot(owner_rows(), per_bucket.astype(bf16), TN)
    whole[:, QKV + HALF :] = jnp.where(tall == AT_ATTN, sums, extra).astype(bf16)


def input_backward(x_ref, grad_after, to_own, got, weights, grad_in):
    gain = gain_row(weights[:, QKV:], AT_ATTN)
    back, _ = norm_backward(x_ref[...].astype(f32), to_own[...] + got[...], gain)
    grad_in[...] = grad_after[...] + back


def sum_groups(own, one, two, three, query, key, value, out, router, attn_gain, ffn_gain, bias):
    total = (own[...].astype(f32) + two[...].astype(f32)) + (
        one[...].astype(f32) + three[...].astype(f32)
    )
    for part, target in enumerate((query, key, value, out)):
        target[:, :HALF] = total[:, part * HALF : (part + 1) * HALF]
        target[:, HALF:] = total[:, SENT + part * HALF : SENT + (part + 1) * HALF]
    extra = total[:, SENT - 128 : SENT] + total[:, 2 * SENT - 128 :]
    same = lax.broadcasted_iota(jnp.int32, (24, 24), 0) == lax.broadcasted_iota(
        jnp.int32, (24, 24), 1
    )

    def row(lane):
        spread = jnp.broadcast_to(extra[:, lane : lane + 1], (24, 24))
        return jnp.sum(jnp.where(same, spread, 0.0), axis=0, keepdims=True)

    router[...] = extra[:, :EXPERTS]
    attn_gain[...] = row(AT_ATTN)
    ffn_gain[...] = row(AT_FFN)
    bias[...] = extra[0:1, AT_BIAS : AT_BIAS + HEADS]


def on_device(
    hidden_in,
    doc_ids,
    routes,
    attn_gain,
    w_query,
    w_key,
    w_value,
    w_out,
    rel_bias,
    ffn_gain,
    w_router,
    w_in,
    w_down,
    out_grad,
):
    place = lax.axis_index("exp").astype(jnp.int32)
    pos = jnp.stack([place // 8, (place // 2) % 4, place % 2])
    group = lax.axis_index("rep").astype(jnp.int32).reshape(1)

    def over_exp(value):
        return lax.all_to_all(value, "exp", split_axis=0, concat_axis=0, tiled=True)

    def over_groups(value):
        return lax.all_gather(value, "rep", axis=0, tiled=True)

    packed, beside = call(
        pack_weights,
        [((EXPERTS, 24, WIDE1), bf16), ((24, WIDE2), bf16)],
        w_query,
        w_key,
        w_value,
        w_out,
        w_router,
        attn_gain.reshape(1, 24),
        ffn_gain.reshape(1, 24),
        rel_bias,
        smem=0,
    )
    weights2 = lax.all_gather(beside, "exp", axis=0, tiled=True)
    weights1 = over_exp(packed).reshape(D, WIDE1)
    x_other = on_exp(hidden_in, SWAP)
    doc_row = jnp.stack([doc_ids, on_exp(doc_ids, SWAP)])
    doc_col = doc_row.reshape(2 * TOK, 1)

    placer, placed_grads = call(
        place_grads,
        [((TOK, SLOTS), bf16), ((SLOTS, D), bf16)],
        routes,
        out_grad,
        smem=0,
        flops=500_000_000,
        bytes_accessed=2_000_000,
    )

    def exchange(value):
        width = value.shape[1]
        return over_exp(value.reshape(EXPERTS, CAP, width)).reshape(SLOTS, width)

    slot_mix = exchange(hold_until(placed_grads, weights1))

    attn_in, projected, probs, att_own, att_send = call(
        attention_forward,
        [
            ((2 * TOK, D), bf16),
            ((2 * TOK, QKV), bf16),
            ((HEADS, TOK, TOK), bf16),
            ((TOK, HALF), bf16),
            ((TOK, HALF), bf16),
        ],
        pos,
        hidden_in,
        x_other,
        doc_col,
        doc_row,
        weights1,
        scratch=[pltpu.VMEM((16, 8, 512), f32)],
        flops=9_000_000_000,
        bytes_accessed=10_000_000,
    )
    att_other = on_exp(att_send, SWAP)
    after, ffn_in, router, gate, outbound = call(
        route_forward,
        [
            ((TOK, D), f32),
            ((TOK, D), bf16),
            ((TOK, 128), f32),
            ((TOK, 1), f32),
            ((SLOTS, WIDE), bf16),
        ],
        pos,
        hidden_in,
        routes,
        att_own,
        att_other,
        placer,
        weights2,
        flops=3_000_000_000,
        bytes_accessed=8_000_000,
    )
    slot_rows = exchange(outbound)
    all_mix = over_groups(hold_until(slot_mix, att_send))
    all_rows = over_groups(slot_rows)
    produced, back = run_expert(slot_rows, slot_mix, w_in, w_down)
    grad_back = exchange(back)
    returned = exchange(produced)

    grad_after, grad_own, grad_send, keep, send = call(
        route_backward,
        [
            ((TOK, D), f32),
            ((TOK, HALF), bf16),
            ((TOK, HALF), bf16),
            ((D, HALF + 128), bf16),
            ((D, HALF), bf16),
        ],
        pos,
        routes,
        out_grad,
        att_own,
        att_other,
        after,
        ffn_in,
        router,
        gate,
        placer,
        grad_back,
        weights2,
        scratch=[pltpu.VMEM((D, D), bf16)],
        flops=4_000_000_000,
        bytes_accessed=10_000_000,
    )
    grad_other = on_exp(grad_send, SWAP)
    got = on_exp(send, SWAP)
    grad_projected, diagonals = call(
        attention_backward,
        [((2 * TOK, QKV), bf16), ((16, 8, 512), f32)],
        pos,
        projected,
        probs,
        grad_own,
        grad_other,
        flops=9_000_000_000,
        bytes_accessed=8_000_000,
    )
    (block_out,) = call(
        mix_out,
        [((TOK, D), bf16)],
        after,
        gate,
        placer,
        returned,
        smem=0,
        flops=200_000_000,
        bytes_accessed=3_000_000,
    )
    whole, to_own, to_send = call(
        weights_backward,
        [((D, SENT), bf16), ((TOK, D), f32), ((TOK, D), f32)],
        hidden_in,
        x_other,
        attn_in,
        grad_projected,
        weights1,
        diagonals,
        keep,
        got,
        smem=0,
        after=[block_out],
        flops=5_000_000_000,
        bytes_accessed=10_000_000,
    )
    parts = over_exp(whole.reshape(EXPERTS, 24, SENT))
    to_got = on_exp(to_send, SWAP)
    grad_w_in, grad_w_down = run_expert_weights(group, all_rows, all_mix, w_in, w_down, to_send)
    (grad_in,) = call(
        input_backward,
        [((TOK, D), f32)],
        hidden_in,
        grad_after,
        to_own,
        to_got,
        weights1,
        smem=0,
        flops=10_000_000,
        bytes_accessed=5_000_000,
    )
    (own,) = call(
        sum_parts, [((24, 2 * SENT), bf16)], parts, smem=0, after=[grad_w_in, grad_in]
    )
    others = [lax.ppermute(own, "rep", z_shift(k)) for k in (1, 2, 3)]
    (
        grad_query,
        grad_key,
        grad_value,
        grad_out,
        grad_router,
        grad_attn_gain,
        grad_ffn_gain,
        grad_rel_bias,
    ) = call(
        sum_groups,
        [((24, D), f32)] * 4
        + [((24, EXPERTS), f32), ((1, 24), f32), ((1, 24), f32), ((1, HEADS), f32)],
        own,
        *others,
        smem=0,
    )
    return (
        block_out,
        grad_in,
        grad_attn_gain.reshape(24),
        grad_query,
        grad_key,
        grad_value,
        grad_out,
        grad_rel_bias,
        grad_ffn_gain.reshape(24),
        grad_router,
        grad_w_in,
        grad_w_down,
    )


def solution(mesh):
    in_specs = (
        P(("rep", "exp"), None),
        P(("rep", "exp")),
        P(("rep", "exp"), None),
        P("exp"),
        P("exp", None),
        P("exp", None),
        P("exp", None),
        P("exp", None),
        P("exp", None),
        P("exp"),
        P("exp", None),
        P("exp", None, None),
        P("exp", None, None),
        P(("rep", "exp"), None),
    )
    out_specs = (
        P(("rep", "exp"), None),
        P(("rep", "exp"), None),
        P("exp"),
        P("exp", None),
        P("exp", None),
        P("exp", None),
        P("exp", None),
        P("exp", None),
        P("exp"),
        P("exp", None),
        P("exp", None, "rep"),
        P("exp", "rep", None),
    )
    return jax.shard_map(
        on_device, mesh=mesh, in_specs=in_specs, out_specs=out_specs, check_vma=False
    )
```

profile of v0, /device:TPU:0, one launch (start us, length us, event | category | flops | bytes accessed | tf_op | source)
XLA Modules:
  0.0 246.1 jit_solution(6309122405466996138)
XLA Ops:
  7.2 2.3 shard_map.229
  9.5 7.4 %all-to-all-start = ((bf16[32,24,1280]{2,1,0:T(8,128)(2,1)}), bf16[32,24,1280]{2,1,0:T(8,128)(2,1)S(1)}, u32[]{:S(2)}, u32[]{:S(2)}) async-start(bf16[32,24,1280]{2,1,0:T(8,128)(2,1)} %get-tuple-element.48), calls=%async_computation | async-start | bytes 3932160 | tf_op jit(solution)/shard_map/all_to_all | solution.py:566
  19.7 2.9 %shard_map.231 = (bf16[256,512]{1,0:T(8,128)(2,1)}, bf16[512,768]{1,0:T(8,128)(2,1)}) custom-call(s32[256,1]{1,0:T(8,128)} %copy.30.refs_0_.refs_2_.refs_1_, bf16[256,768]{1,0:T(8,128)(2,1)} %refs_2_.5), custom_call_target="tpu_custom_call" | custom-call | flops 500000000 | bytes 2000000 | tf_op jit(solution)/shard_map/pallas_call | solution.py:68
  24.0 21.6 %all-to-all-done = bf16[32,24,1280]{2,1,0:T(8,128)(2,1)S(1)} async-done(((bf16[32,24,1280]{2,1,0:T(8,128)(2,1)}), bf16[32,24,1280]{2,1,0:T(8,128)(2,1)S(1)}, u32[]{:S(2)}, u32[]{:S(2)}) %all-to-all-start) | async-done | bytes 1966112 | tf_op jit(solution)/shard_map/all_to_all | solution.py:566
  46.8 3.9 %all-to-all-start.2 = ((bf16[32,16,768]{2,1,0:T(8,128)(2,1)}), bf16[32,16,768]{2,1,0:T(8,128)(2,1)S(1)}, u32[]{:S(2)}, u32[]{:S(2)}) async-start(bf16[32,16,768]{2,1,0:T(8,128)(2,1)} %bitcast.33), calls=%async_computation.2 | async-start | bytes 1572864 | tf_op jit(solution)/shard_map/all_to_all | solution.py:566
  51.5 11.3 %shard_map.230 = (bf16[512,768]{1,0:T(8,128)(2,1)}, bf16[512,1152]{1,0:T(8,128)(2,1)}, bf16[12,256,256]{2,1,0:T(8,128)(2,1)}, bf16[256,384]{1,0:T(8,128)(2,1)}, bf16[256,384]{1,0:T(8,128)(2,1)}) custom-call(s32[3]{0:T(128)} %pad_add_fusion.1.refs_0_, bf16[256,768]{1,0:T(8,128)(2,1)} %refs_0_.6, bf16[256,768]{1,0:T(8,128)(2,1)} %copy-done.14, ...), custom_call_target="tpu_custom_call" | custom-call | flops 8999999488 | bytes 10000000 | tf_op jit(solution)/shard_map/pallas_call | solution.py:68
  64.4 9.1 %all-gather.4.cloned.1.call-done.refs_6_.refs_11_ = bf16[768,896]{1,0:T(8,128)(2,1)} async-done(((bf16[24,896]{1,0:T(8,128)(2,1)}), bf16[768,896]{1,0:T(8,128)(2,1)}) %all-gather.4.cloned.1.call-update) | async-done | bytes 1376272 | tf_op jit(solution)/shard_map/all_gather | solution.py:584
  73.5 4.4 %shard_map.232 = (f32[256,768]{1,0:T(8,128)}, bf16[256,768]{1,0:T(8,128)(2,1)}, f32[256,128]{1,0:T(8,128)}, f32[256,1]{1,0:T(8,128)}, bf16[512,896]{1,0:T(8,128)(2,1)}) custom-call(s32[3]{0:T(128)} %pad_add_fusion.1.refs_0_, bf16[256,768]{1,0:T(8,128)(2,1)} %refs_0_.6, s32[256,1]{1,0:T(8,128)} %copy.30.refs_0_.refs_2_.refs_1_, ...), custom_call_target="tpu_custom_call" | custom-call | flops 3000000000 | bytes 8000000 | tf_op jit(solution)/shard_map/pallas_call | solution.py:68
  77.9 21.1 %all_to_all.30 = bf16[32,16,896]{2,1,0:T(8,128)(2,1)} all-to-all(bf16[32,16,896]{2,1,0:T(8,128)(2,1)} %bitcast.38), channel_id=1, replica_groups=mesh['rep'=4,'exp'=32] {'exp'}, dimensions={0} | all-to-all | bytes 1835008 | tf_op jit(solution)/shard_map/all_to_all | solution.py:566
  99.0 17.5 %shard_map.234 = (bf16[512,768]{1,0:T(8,128)(2,1)}, bf16[512,896]{1,0:T(8,128)(2,1)}) custom-call(bf16[512,896]{1,0:T(8,128)(2,1)} %bitcast.31, bf16[512,768]{1,0:T(8,128)(2,1)} %bitcast.29, bf16[1,768,3072]{2,1,0:T(8,128)(2,1)} %refs_2_.6, bf16[1,3072,768]{2,1,0:T(8,128)(2,1)} %refs_3_.3), custom_call_target="tpu_custom_call" | custom-call | flops 9663676416 | bytes 14680064 | tf_op jit(solution)/shard_map/pallas_call | solution.py:342
  117.9 19.6 %all_to_all.31 = bf16[32,16,896]{2,1,0:T(8,128)(2,1)} all-to-all(bf16[32,16,896]{2,1,0:T(8,128)(2,1)S(1)} %bitcast.36), channel_id=1, replica_groups=mesh['rep'=4,'exp'=32] {'exp'}, dimensions={0} | all-to-all | bytes 1835008 | tf_op jit(solution)/shard_map/all_to_all | solution.py:566
  137.5 4.1 %all-to-all-start.3 = ((bf16[32,16,768]{2,1,0:T(8,128)(2,1)}), bf16[32,16,768]{2,1,0:T(8,128)(2,1)S(1)}, u32[]{:S(2)}, u32[]{:S(2)}) async-start(bf16[32,16,768]{2,1,0:T(8,128)(2,1)} %bitcast.12), calls=%async_computation.3 | async-start | bytes 1572864 | tf_op jit(solution)/shard_map/all_to_all | solution.py:566
  141.6 6.4 %shard_map.236 = (f32[256,768]{1,0:T(8,128)}, bf16[256,384]{1,0:T(8,128)(2,1)}, bf16[256,384]{1,0:T(8,128)(2,1)}, bf16[768,512]{1,0:T(8,128)(2,1)}, bf16[768,384]{1,0:T(8,128)(2,1)}) custom-call(s32[3]{0:T(128)} %pad_add_fusion.1.refs_0_, s32[256,1]{1,0:T(8,128)} %copy.30.refs_0_.refs_2_.refs_1_, bf16[256,768]{1,0:T(8,128)(2,1)} %refs_2_.5, ...), custom_call_target="tpu_custom_call" | custom-call | flops 4000000000 | bytes 10000000 | tf_op jit(solution)/shard_map/pallas_call | solution.py:68
  148.0 7.9 %all-to-all-done.3 = bf16[32,16,768]{2,1,0:T(8,128)(2,1)S(1)} async-done(((bf16[32,16,768]{2,1,0:T(8,128)(2,1)}), bf16[32,16,768]{2,1,0:T(8,128)(2,1)S(1)}, u32[]{:S(2)}, u32[]{:S(2)}) %all-to-all-start.3) | async-done | bytes 786464 | tf_op jit(solution)/shard_map/all_to_all | solution.py:566
  156.9 2.6 %shard_map.235.refs_8_ = bf16[256,768]{1,0:T(8,128)(2,1)} custom-call(f32[256,768]{1,0:T(8,128)} %get-tuple-element.53.refs_0_.refs_5_, f32[256,1]{1,0:T(8,128)} %get-tuple-element.54.refs_1_.refs_8_, bf16[256,512]{1,0:T(8,128)(2,1)} %get-tuple-element.51.refs_5_.refs_2_.refs_9_, bf16[512,768]{1,0:T(8,128)(2,1)} %bitcast.34), custom_call_target="tpu_custom_call" | custom-call | flops 200000000 | bytes 3000000 | tf_op jit(solution)/shard_map/pallas_call | solution.py:68
  160.2 7.7 %shard_map.237 = (bf16[512,1152]{1,0:T(8,128)(2,1)}, f32[16,8,512]{2,1,0:T(8,128)}) custom-call(s32[3]{0:T(128)} %pad_add_fusion.1.refs_0_, bf16[512,1152]{1,0:T(8,128)(2,1)} %get-tuple-element.63.refs_1_, bf16[12,256,256]{2,1,0:T(8,128)(2,1)} %get-tuple-element.64.refs_2_, bf16[256,384]{1,0:T(8,128)(2,1)} %get-tuple-element.65.refs_3_, ...), custom_call_target="tpu_custom_call" | custom-call | flops 8999999488 | bytes 8000000 | tf_op jit(solution)/shard_map/pallas_call | solution.py:68
  168.8 10.2 %shard_map.238 = (bf16[768,1664]{1,0:T(8,128)(2,1)}, f32[256,768]{1,0:T(8,128)}, f32[256,768]{1,0:T(8,128)}) custom-call(bf16[256,768]{1,0:T(8,128)(2,1)} %refs_0_.6, bf16[256,768]{1,0:T(8,128)(2,1)} %copy-done.14, bf16[512,768]{1,0:T(8,128)(2,1)} %get-tuple-element.62.refs_2_, bf16[512,1152]{1,0:T(8,128)(2,1)} %get-tuple-element.67.refs_3_, ...), custom_call_target="tpu_custom_call" | custom-call | flops 5000000000 | bytes 10000000 | tf_op jit(solution)/shard_map/pallas_call | solution.py:68
  179.0 4.1 %all-to-all-start.5 = ((bf16[32,24,1664]{2,1,0:T(8,128)(2,1)}), bf16[32,24,1664]{2,1,0:T(8,128)(2,1)S(1)}, u32[]{:S(2)}, u32[]{:S(2)}) async-start(bf16[32,24,1664]{2,1,0:T(8,128)(2,1)} %bitcast.35), calls=%async_computation.5 | async-start | bytes 5111808 | tf_op jit(solution)/shard_map/all_to_all | solution.py:566
  186.8 3.7 %shard_map.239.refs_2_ = f32[256,768]{1,0:T(8,128)} custom-call(bf16[256,768]{1,0:T(8,128)(2,1)} %refs_0_.6, f32[256,768]{1,0:T(8,128)} %get-tuple-element.61.refs_1_, f32[256,768]{1,0:T(8,128)} %get-tuple-element.71.refs_2_, f32[256,768]{1,0:T(8,128)} %copy-done.5, bf16[768,1280]{1,0:T(8,128)(2,1)} %bitcast.28), custom_call_target="tpu_custom_call" | custom-call | flops 10000000 | bytes 5000000 | tf_op jit(solution)/shard_map/pallas_call | solution.py:68
  190.5 12.5 %all-gather.6.cloned.1.call-done.refs_0_ = bf16[2048,896]{1,0:T(8,128)(2,1)} async-done(((bf16[512,896]{1,0:T(8,128)(2,1)}), bf16[2048,896]{1,0:T(8,128)(2,1)}) %all-gather.6.cloned.1.call-update) | async-done | bytes 3670032 | tf_op jit(solution)/shard_map/all_gather | solution.py:569
  203.0 18.3 %shard_map.241 = (f32[1,768,768]{2,1,0:T(8,128)}, f32[1,768,768]{2,1,0:T(8,128)}) custom-call(s32[1]{0:T(128)} %bitcast.17.pos, bf16[2048,896]{1,0:T(8,128)(2,1)} %all-gather.6.cloned.1.call-done.refs_0_, bf16[2048,768]{1,0:T(8,128)(2,1)} %all-gather.8.cloned.1.call-done.refs_1_, bf16[1,768,3072]{2,1,0:T(8,128)(2,1)} %refs_2_.6, ...), custom_call_target="tpu_custom_call" | custom-call | flops 9663676416 | bytes 14680064 | tf_op jit(solution)/shard_map/pallas_call | solution.py:370
  222.8 2.7 %shard_map.242.refs_0_ = bf16[24,3328]{1,0:T(8,128)(2,1)} custom-call(bf16[32,24,1664]{2,1,0:T(8,128)(2,1)} %copy-done.1, f32[1,768,768]{2,1,0:T(8,128)} %get-tuple-element.46.refs_1_, f32[256,768]{1,0:T(8,128)} %shard_map.239.refs_2_), custom_call_target="tpu_custom_call" | custom-call | tf_op jit(solution)/shard_map/pallas_call | solution.py:68
  227.8 2.4 collective-permute-start.8
  230.1 6.1 %collective-permute-done.6.refs_1_ = bf16[24,3328]{1,0:T(8,128)(2,1)S(1)} collective-permute-done((bf16[24,3328]{1,0:T(8,128)(2,1)}, bf16[24,3328]{1,0:T(8,128)(2,1)S(1)}, u32[]{:S(2)}, u32[]{:S(2)}) %collective-permute-start.6) | collective-permute-done | bytes 159776 | tf_op jit(solution)/shard_map/ppermute | solution.py:735
  (67 shorter events, 22.4 us)
Async XLA Ops:
  7.2 10.5 %copy-start.6 = (bf16[256,768]{1,0:T(8,128)(2,1)S(1)}, bf16[256,768]{1,0:T(8,128)(2,1)}, u32[]{:S(2)}) copy-start(bf16[256,768]{1,0:T(8,128)(2,1)} %refs_0_.6) | copy-start | bytes 1179652
  7.2 10.8 %copy-start.11 = (s32[256]{0:T(256)S(1)}, s32[256]{0:T(256)}, u32[]{:S(2)}) copy-start(s32[256]{0:T(256)} %param.15) | copy-start | bytes 3076
  7.2 11.1 %copy-start.10 = (s32[256,1]{0,1:T(1,128)S(1)}, s32[256,1]{0,1:T(1,128)}, u32[]{:S(2)}) copy-start(s32[256,1]{0,1:T(1,128)} %param.16) | copy-start | bytes 3076
  9.5 36.0 %all-to-all-start = ((bf16[32,24,1280]{2,1,0:T(8,128)(2,1)}), bf16[32,24,1280]{2,1,0:T(8,128)(2,1)S(1)}, u32[]{:S(2)}, u32[]{:S(2)}) async-start(bf16[32,24,1280]{2,1,0:T(8,128)(2,1)} %get-tuple-element.48), calls=%async_computation | async-start | bytes 3932160 | tf_op jit(solution)/shard_map/all_to_all | solution.py:566
  16.9 56.5 %all-gather.4.cloned.1.call-start = ((), (), s32[]{:S(2)}) async-start(), calls=%async_computation.6 | async-start | bytes 1419264 | tf_op jit(solution)/shard_map/all_gather | solution.py:584
  17.7 33.1 %collective-permute-start = (bf16[256,768]{1,0:T(8,128)(2,1)S(1)}, bf16[256,768]{1,0:T(8,128)(2,1)S(1)}, u32[]{:S(2)}, u32[]{:S(2)}) collective-permute-start(bf16[256,768]{1,0:T(8,128)(2,1)S(1)} %copy-done.6), channel_id=1, source_target_pairs={{0,1},{1,0},{2,3},{3,2},{4,5},{5,4},{6,7},{7,6},{8,9},{9,8},{10,11... | collective-permute-start | bytes 1179656 | tf_op jit(solution)/shard_map/ppermute | solution.py:48
  18.0 4.5 %collective-permute-start.1 = (s32[256]{0:T(256)S(1)}, s32[256]{0:T(256)S(1)}, u32[]{:S(2)}, u32[]{:S(2)}) collective-permute-start(s32[256]{0:T(256)S(1)} %copy-done.11), channel_id=1, source_target_pairs={{0,1},{1,0},{2,3},{3,2},{4,5},{5,4},{6,7},{7,6},{8,9},{9,8},{10,11... | collective-permute-start | bytes 3080 | tf_op jit(solution)/shard_map/ppermute | solution.py:48
  46.8 31.1 %all-to-all-start.2 = ((bf16[32,16,768]{2,1,0:T(8,128)(2,1)}), bf16[32,16,768]{2,1,0:T(8,128)(2,1)S(1)}, u32[]{:S(2)}, u32[]{:S(2)}) async-start(bf16[32,16,768]{2,1,0:T(8,128)(2,1)} %bitcast.33), calls=%async_computation.2 | async-start | bytes 1572864 | tf_op jit(solution)/shard_map/all_to_all | solution.py:566
  62.8 1.7 collective-permute-start.2
  64.4 9.1 %copy-start.15 = (bf16[256,384]{1,0:T(8,128)(2,1)}, bf16[256,384]{1,0:T(8,128)(2,1)S(1)}, u32[]{:S(2)}) copy-start(bf16[256,384]{1,0:T(8,128)(2,1)S(1)} %collective-permute-done.2.refs_4_) | copy-start | bytes 589828
  77.9 21.1 %copy-start.2 = (bf16[32,16,768]{2,1,0:T(8,128)(2,1)}, bf16[32,16,768]{2,1,0:T(8,128)(2,1)S(1)}, u32[]{:S(2)}) copy-start(bf16[32,16,768]{2,1,0:T(8,128)(2,1)S(1)} %all-to-all-done.2) | copy-start | bytes 2359300
  116.4 1.5 copy-start.4
  116.4 74.0 %all-gather.8.cloned.1.call-start = ((), (), s32[]{:S(2)}) async-start(), calls=%async_computation.8 | async-start | bytes 3932160 | tf_op jit(solution)/shard_map/all_gather | solution.py:569
  117.2 85.8 %all-gather.6.cloned.1.call-start = ((), (), s32[]{:S(2)}) async-start(), calls=%async_computation.7 | async-start | bytes 4587520 | tf_op jit(solution)/shard_map/all_gather | solution.py:569
  137.5 18.5 %all-to-all-start.3 = ((bf16[32,16,768]{2,1,0:T(8,128)(2,1)}), bf16[32,16,768]{2,1,0:T(8,128)(2,1)S(1)}, u32[]{:S(2)}, u32[]{:S(2)}) async-start(bf16[32,16,768]{2,1,0:T(8,128)(2,1)} %bitcast.12), calls=%async_computation.3 | async-start | bytes 1572864 | tf_op jit(solution)/shard_map/all_to_all | solution.py:566
  148.0 11.5 %copy-start.12 = (bf16[768,384]{1,0:T(8,128)(2,1)S(1)}, bf16[768,384]{1,0:T(8,128)(2,1)}, u32[]{:S(2)}) copy-start(bf16[768,384]{1,0:T(8,128)(2,1)} %get-tuple-element.70) | copy-start | bytes 1769476
  148.0 11.5 %collective-permute-start.3 = (bf16[256,384]{1,0:T(8,128)(2,1)}, bf16[256,384]{1,0:T(8,128)(2,1)S(1)}, u32[]{:S(2)}, u32[]{:S(2)}) collective-permute-start(bf16[256,384]{1,0:T(8,128)(2,1)} %get-tuple-element.66), channel_id=1, source_target_pairs={{0,1},{1,0},{2,3},{3,2},{4,5},{5,4},{6,7},{7,6},{8,9},{9,8},{10,11... | collective-permute-start | bytes 589832 | tf_op jit(solution)/shard_map/ppermute | solution.py:48
  159.6 8.4 %collective-permute-start.4 = (bf16[768,384]{1,0:T(8,128)(2,1)S(1)}, bf16[768,384]{1,0:T(8,128)(2,1)S(1)}, u32[]{:S(2)}, u32[]{:S(2)}) collective-permute-start(bf16[768,384]{1,0:T(8,128)(2,1)S(1)} %copy-done.12), channel_id=1, source_target_pairs={{0,1},{1,0},{2,3},{3,2},{4,5},{5,4},{6,7},{7,6},{8,9},{9,8},{10,11... | collective-permute-start | bytes 1769480 | tf_op jit(solution)/shard_map/ppermute | solution.py:48
  179.0 42.3 %all-to-all-start.5 = ((bf16[32,24,1664]{2,1,0:T(8,128)(2,1)}), bf16[32,24,1664]{2,1,0:T(8,128)(2,1)S(1)}, u32[]{:S(2)}, u32[]{:S(2)}) async-start(bf16[32,24,1664]{2,1,0:T(8,128)(2,1)} %bitcast.35), calls=%async_computation.5 | async-start | bytes 5111808 | tf_op jit(solution)/shard_map/all_to_all | solution.py:566
  183.1 2.8 %collective-permute-start.5 = (f32[256,768]{1,0:T(8,128)}, f32[256,768]{1,0:T(8,128)S(1)}, u32[]{:S(2)}, u32[]{:S(2)}) collective-permute-start(f32[256,768]{1,0:T(8,128)} %get-tuple-element.72.refs_4_), channel_id=1, source_target_pairs={{0,1},{1,0},{2,3},{3,2},{4,5},{5,4},{6,7},{7,6},{8,9},{9,8},{10,11... | collective-permute-start | bytes 2359304 | tf_op jit(solution)/shard_map/ppermute | solution.py:48
  221.4 1.4 copy-start.1
  225.5 10.7 %collective-permute-start.6 = (bf16[24,3328]{1,0:T(8,128)(2,1)}, bf16[24,3328]{1,0:T(8,128)(2,1)S(1)}, u32[]{:S(2)}, u32[]{:S(2)}) collective-permute-start(bf16[24,3328]{1,0:T(8,128)(2,1)} %shard_map.242.refs_0_), channel_id=1, source_target_pairs={{0,32},{32,64},{64,96},{96,0},{1,33},{33,65},{65,97},{97,1},{2,34}... | collective-permute-start | bytes 479240 | tf_op jit(solution)/shard_map/ppermute | solution.py:735
  226.2 10.0 %collective-permute-start.7 = (bf16[24,3328]{1,0:T(8,128)(2,1)}, bf16[24,3328]{1,0:T(8,128)(2,1)S(1)}, u32[]{:S(2)}, u32[]{:S(2)}) collective-permute-start(bf16[24,3328]{1,0:T(8,128)(2,1)} %shard_map.242.refs_0_), channel_id=1, source_target_pairs={{0,64},{32,96},{64,0},{96,32},{1,65},{33,97},{65,1},{97,33},{2,66}... | collective-permute-start | bytes 479240 | tf_op jit(solution)/shard_map/ppermute | solution.py:735
  227.8 9.0 %collective-permute-start.8 = (bf16[24,3328]{1,0:T(8,128)(2,1)}, bf16[24,3328]{1,0:T(8,128)(2,1)S(1)}, u32[]{:S(2)}, u32[]{:S(2)}) collective-permute-start(bf16[24,3328]{1,0:T(8,128)(2,1)} %shard_map.242.refs_0_), channel_id=1, source_target_pairs={{0,96},{32,0},{64,32},{96,64},{1,97},{33,1},{65,33},{97,65},{2,98}... | collective-permute-start | bytes 479240 | tf_op jit(solution)/shard_map/ppermute | solution.py:735
  (9 other events, 7.4 us)
Sparse Core Ops, SparseCore 0:
  20.7 52.7 all-gather.3
  118.9 38.1 all-gather.7
  158.8 44.1 all-gather.5
where the time goes:
time: 247 us; the launch traced here: 246 us
  Pallas kernels  92 us (37%)
  waiting for transfers between devices  63.6 us (26%)
  blocking collectives  40.7 us (16%)
  starting transfers between devices  25.5 us (10%)
  between operations  13.9 us (6%)
  local copies, waits for them, and re-layouts  9.29 us (4%)
    pallas_call x11, Pallas kernels, call(): pl.pallas_call(run, out_shape=[jax.ShapeDtypeStruct(shape, kind) for shap...  56.2 us
    all_to_all x2, blocking collectives, over_exp(): return lax.all_to_all(value, 'exp', split_axis=0, concat_axis=0, tiled=True)  40.7 us
    all_to_all x4, waiting for transfers between devices, over_exp(): return lax.all_to_all(value, 'exp', split_axis=0, concat_axis=0, tiled=True)  29.5 us
    all_to_all x4, starting transfers between devices, over_exp(): return lax.all_to_all(value, 'exp', split_axis=0, concat_axis=0, tiled=True)  19.5 us
    pallas_call x1, Pallas kernels, run_expert_weights(): pl.pallas_call(expert_weights, grid_spec=pltpu.PrefetchScalarGridSpec(num...  18.3 us
    pallas_call x1, Pallas kernels, run_expert(): pl.pallas_call(expert_block, grid=(FF // BLOCK,), in_specs=[wide, whole,...  17.5 us
    all_gather x2, waiting for transfers between devices, over_groups(): return lax.all_gather(value, 'rep', axis=0, tiled=True)  12.5 us
    unnamed x37, local copies, waits for them, and re-layouts  9.29 us
  transfers between devices with their start and end apart: 16, of which 8 were waited for; matrix products, arithmetic and copies ran while one was open for 1% of the time, Pallas kernels for 27%

commit v1 on v0

--- a/solution.py
+++ b/solution.py
@@ -16,8 +16,6 @@
 SLOTS = EXPERTS * CAP
 HALF = D // 2
 QKV = 3 * HALF
-WIDE1 = QKV + 128
-WIDE2 = D + 128
 WIDE = D + 128
 SENT = QKV + HALF + 128
 AT_FFN = EXPERTS
@@ -78,7 +76,7 @@
     )(*args, *after)
 
 
-def pack_weights(query, key, value, out, router, attn_gain, ffn_gain, bias, packed, beside):
+def pack_weights(query, key, value, out, router, attn_gain, ffn_gain, bias, packed):
     same = lax.broadcasted_iota(jnp.int32, (24, 24), 0) == lax.broadcasted_iota(
         jnp.int32, (24, 24), 1
     )
@@ -99,12 +97,10 @@
         ],
         axis=1,
     ).astype(bf16)
-    beside[:, :D] = out[...]
-    beside[:, D:] = extra
     for core in range(2):
         columns = slice(core * HALF, (core + 1) * HALF)
         half = jnp.concatenate(
-            [query[:, columns], key[:, columns], value[:, columns], extra], axis=1
+            [query[:, columns], key[:, columns], value[:, columns], out[:, columns], extra], axis=1
         )
         for chip in range(16):
             packed[2 * chip + core] = half
@@ -150,8 +146,10 @@
 
 
 def attention_forward(pos, x_own, x_other, doc_col, doc_row, weights, *refs):
-    attn_in, projected, probs, attended_own, attended_other, base = refs
-    extra = weights[:, QKV:]
+    extras, out_half, attn_in, projected, probs, attended_own, attended_other, base = refs
+    extra = weights[:, SENT - 128 :]
+    extras[...] = extra
+    out_half[...] = weights[:, QKV : QKV + HALF]
     gain = gain_row(extra, AT_ATTN)
     head = lax.broadcasted_iota(jnp.int32, (128, 16), 1)
     moved = (lax.broadcasted_iota(jnp.int32, (128, 16), 0) == head + AT_BIAS).astype(bf16)
@@ -247,15 +245,17 @@
     return own, other
 
 
-def route_forward(pos, x_ref, routes, att_own, att_other, placer, weights, *refs):
-    after, ffn_in, router, gate, outbound = refs
+def route_forward(pos, x_ref, routes, att_own, att_other, placer, out_half, out_got, extras, *refs):
+    weights, after, ffn_in, router, gate, outbound = refs
     own, other = core_halves(pos)
-    extra = weights[:, D:]
+    weights[:, own] = out_half[...]
+    weights[:, other] = out_got[...]
+    extra = extras[...]
     gain = gain_row(extra, AT_FFN)
     after_attn = (
         x_ref[...].astype(f32)
-        + dot(att_own[...], weights[own, :D], NN)
-        + dot(att_other[...], weights[other, :D], NN)
+        + dot(att_own[...], weights[own, :], NN)
+        + dot(att_other[...], weights[other, :], NN)
     )
     after[...] = after_attn
     ffn_input = (after_attn * inverse_rms(after_attn) * gain).astype(bf16)
@@ -274,11 +274,10 @@
 
 def gelu_parts(pre):
     square = pre * pre
-    inner = 0.7978845608028654 * pre * (1.0 + 0.044715 * square)
-    bend = jnp.tanh(inner)
-    cdf = 0.5 * (1.0 + bend)
-    slope = cdf + 0.5 * pre * (1.0 - bend * bend) * (
-        0.7978845608028654 * (1.0 + 0.134145 * square)
+    bend = jnp.tanh(pre * (0.7978845608028654 + 0.035677408136300125 * square))
+    cdf = 0.5 + 0.5 * bend
+    slope = cdf + (pre - pre * (bend * bend)) * (
+        0.3989422804014327 + 0.05351611220445019 * square
     )
     return pre * cdf, slope
 
@@ -314,40 +313,50 @@
         back[:, D:] = in_parts(per_gate, SLOTS)
 
 
-def expert_weights(pos, *refs):
-    all_rows, all_mix, w_in, w_down, _, grad_in, grad_down = refs
-    for k in range(4):
-        group = slice(k * SLOTS, (k + 1) * SLOTS)
-        own = all_rows[group, :D]
-        grads = (from_parts(all_rows[group, D:]) * all_mix[group].astype(f32)).astype(bf16)
+def expert_weights(pos, count, *refs):
+    rows, mix = refs[:count], refs[count : 2 * count]
+    w_in, w_down = refs[2 * count : 2 * count + 2]
+    grad_in, grad_down = refs[-2:]
+    kept = refs[2 * count + 2 : -3]
+    for k in range(count):
+        own = rows[k][:, :D]
+        grads = (from_parts(rows[k][:, D:]) * mix[k][...].astype(f32)).astype(bf16)
         active, slope = gelu_parts(dot(own, w_in[0], NN))
         grad_pre = (dot(grads, w_down[0], NT) * slope).astype(bf16)
         to_in = dot(own, grad_pre, TN)
         to_down = dot(active.astype(bf16), grads, TN)
-        if k == 0:
+        if k > 0:
+            grad_in[0] += to_in
+            grad_down[0] += to_down
+        elif kept:
+            grad_in[0] = kept[0][0] + to_in
+            grad_down[0] = kept[1][0] + to_down
+        else:
             grad_in[0] = to_in
             grad_down[0] = to_down
-        else:
-            grad_in[0] += to_in
-            grad_down[0] += to_down
 
 
 BLOCK = 512
 WBLOCK = 256
 
 
-def run_expert(rows, mix, w_in, w_down):
+def run_expert(rows, mix, w_in, w_down, after):
     wide = pl.BlockSpec((SLOTS, WIDE), lambda f: (0, 0))
     whole = pl.BlockSpec((SLOTS, D), lambda f: (0, 0))
+
+    def run(*refs):
+        expert_block(*refs[:4], *refs[4 + len(after) :])
+
     return pl.pallas_call(
-        expert_block,
+        run,
         grid=(FF // BLOCK,),
         in_specs=[
             wide,
             whole,
             pl.BlockSpec((1, D, BLOCK), lambda f: (0, 0, f)),
             pl.BlockSpec((1, BLOCK, D), lambda f: (0, f, 0)),
-        ],
+        ]
+        + [pl.BlockSpec(memory_space=pl.ANY) for _ in after],
         out_specs=[whole, wide],
         out_shape=[
             jax.ShapeDtypeStruct((SLOTS, D), bf16),
@@ -362,37 +371,42 @@
         cost_estimate=pl.CostEstimate(
             flops=8 * SLOTS * D * FF, bytes_accessed=14 * 1024 * 1024, transcendentals=0
         ),
-    )(rows, mix, w_in, w_down)
-
-
-def run_expert_weights(group, rows, mix, w_in, w_down, after):
-    steps = D // WBLOCK
+    )(rows, mix, w_in, w_down, *after)
+
+
+def run_expert_weights(group, rows, mix, w_in, w_down, kept, after):
+    steps, count = D // WBLOCK, len(rows)
+    own_in = pl.BlockSpec((1, D, WBLOCK), lambda f, g: (0, 0, f))
+    own_down = pl.BlockSpec((1, WBLOCK, D), lambda f, g: (0, f, 0))
+
+    def run(pos, *refs):
+        expert_weights(pos, count, *refs)
+
     return pl.pallas_call(
-        expert_weights,
+        run,
         grid_spec=pltpu.PrefetchScalarGridSpec(
             num_scalar_prefetch=1,
             grid=(steps,),
             in_specs=[
-                pl.BlockSpec((4 * SLOTS, WIDE), lambda f, g: (0, 0)),
-                pl.BlockSpec((4 * SLOTS, D), lambda f, g: (0, 0)),
+                *[pl.BlockSpec((SLOTS, WIDE), lambda f, g: (0, 0))] * count,
+                *[pl.BlockSpec((SLOTS, D), lambda f, g: (0, 0))] * count,
                 pl.BlockSpec((1, D, WBLOCK), lambda f, g: (0, 0, g[0] * steps + f)),
                 pl.BlockSpec((1, WBLOCK, D), lambda f, g: (0, g[0] * steps + f, 0)),
+                *[own_in, own_down][: len(kept)],
                 pl.BlockSpec(memory_space=pl.ANY),
             ],
-            out_specs=[
-                pl.BlockSpec((1, D, WBLOCK), lambda f, g: (0, 0, f)),
-                pl.BlockSpec((1, WBLOCK, D), lambda f, g: (0, f, 0)),
-            ],
+            out_specs=[own_in, own_down],
         ),
         out_shape=[
             jax.ShapeDtypeStruct((1, D, D), f32),
             jax.ShapeDtypeStruct((1, D, D), f32),
         ],
+        input_output_aliases={2 * count + 3 + i: i for i in range(len(kept))},
         compiler_params=pltpu.CompilerParams(vmem_limit_bytes=60 * 1024 * 1024),
         cost_estimate=pl.CostEstimate(
-            flops=32 * SLOTS * D * D, bytes_accessed=14 * 1024 * 1024, transcendentals=0
+            flops=8 * count * SLOTS * D * D, bytes_accessed=14 * 1024 * 1024, transcendentals=0
         ),
-    )(group, rows, mix, w_in, w_down, after)
+    )(group, *rows, *mix, w_in, w_down, *kept, after)
 
 
 def mix_out(after, gate, placer, returned, block_out):
@@ -410,13 +424,15 @@
 
 
 def column_sums(values):
-    return dot(values, jnp.ones((values.shape[0], 128), f32), TN, HIGHEST)
+    line = jnp.broadcast_to(jnp.sum(values, axis=0, keepdims=True), (8, values.shape[1]))
+    first = lax.broadcasted_iota(jnp.int32, (8, 128), 0) == 0
+    return dot(line, first.astype(f32), TN, HIGHEST)
 
 
 def route_backward(pos, *refs):
-    (routes, out_grad, att_own, att_other, after, ffn_in, router, gate, placer, grad_back, weights) = refs[:11]
-    grad_after, grad_own, grad_other, keep, send, whole = refs[11:]
-    extra_weights = weights[:, D:]
+    (routes, out_grad, att_own, att_other, after, ffn_in, router, gate, placer, grad_back, weights, extras) = refs[:12]
+    grad_after, grad_own, grad_other, keep, send, whole = refs[12:]
+    extra_weights = extras[...]
     gain = gain_row(extra_weights, AT_FFN)
     grad_mix = out_grad[...].astype(f32)
     after_attn = after[...]
@@ -434,8 +450,8 @@
     grad_after[...] = grad_after_attn
     branch = grad_after_attn.astype(bf16)
     own, other = core_halves(pos)
-    grad_own[...] = dot(branch, weights[own, :D], NT).astype(bf16)
-    grad_other[...] = dot(branch, weights[other, :D], NT).astype(bf16)
+    grad_own[...] = dot(branch, weights[own, :], NT).astype(bf16)
+    grad_other[...] = dot(branch, weights[other, :], NT).astype(bf16)
     whole[own, :] = dot(att_own[...], branch, TN).astype(bf16)
     whole[other, :] = dot(att_other[...], branch, TN).astype(bf16)
     keep[:, :HALF] = whole[:, own]
@@ -449,46 +465,47 @@
     left = lax.broadcasted_iota(jnp.int32, (TOK, 128), 1) < 64
     diagonals[...] = jnp.zeros_like(diagonals)
     first_head = pos[2] * (HEADS // 2)
-    for block, grad_att in enumerate((grad_own, grad_other)):
-        rows = slice(block * TOK, (block + 1) * TOK)
-
-        def pair_step(pair, carry):
-            start = pair * 128
-            at_query = pl.ds(pl.multiple_of(start, 128), 128)
-            at_key = pl.ds(pl.multiple_of(start + HALF, 128), 128)
-            at_value = pl.ds(pl.multiple_of(start + 2 * HALF, 128), 128)
-            queries, keys, values = (
-                projected[rows, at_query],
-                projected[rows, at_key],
-                projected[rows, at_value],
-            )
-            grads = grad_att[:, at_query]
-            to_query, to_key, to_value = [], [], []
-            for side in range(2):
-                mine = left if side == 0 else jnp.logical_not(left)
+    blocks = [slice(block * TOK, (block + 1) * TOK) for block in range(2)]
+
+    def pair_step(pair, carry):
+        start = pair * 128
+        at_query = pl.ds(pl.multiple_of(start, 128), 128)
+        at_key = pl.ds(pl.multiple_of(start + HALF, 128), 128)
+        at_value = pl.ds(pl.multiple_of(start + 2 * HALF, 128), 128)
+        to_query, to_key, to_value = [[], []], [[], []], [[], []]
+        for side in range(2):
+            mine = left if side == 0 else jnp.logical_not(left)
+            both = jnp.zeros((TOK, TOK), f32)
+            for block, rows in enumerate(blocks):
+                grads = (grad_own, grad_other)[block][:, at_query]
                 own = jnp.where(mine, grads, jnp.zeros_like(grads))
                 share16 = probs[block * (HEADS // 2) + 2 * pair + side]
                 share = share16.astype(f32)
-                grad_probs = dot(own, values, NT)
-                to_value.append(dot(share16, grads, TN))
+                grad_probs = dot(own, projected[rows, at_value], NT)
+                to_value[block].append(dot(share16, grads, TN))
                 mixed = share * grad_probs
                 grad_scores = mixed - share * jnp.sum(mixed, axis=-1, keepdims=True)
                 grad16 = grad_scores.astype(bf16)
-                to_query.append(dot(grad16, keys, NN))
-                to_key.append(dot(grad16, queries, TN))
-                rounded = grad16.astype(f32)
-                total = jnp.zeros((8, 512), f32)
-                blank = jnp.zeros((8, 256), f32)
-                for g in range(32):
-                    lines = jnp.concatenate([rounded[8 * g : 8 * g + 8], blank], axis=1)
-                    total = total + pltpu.roll(lines, 255 - 8 * g, 1)
-                diagonals[first_head + 2 * pair + side] += total
-            grad_projected[rows, at_query] = (score_scale * jnp.where(left, *to_query)).astype(bf16)
-            grad_projected[rows, at_key] = (score_scale * jnp.where(left, *to_key)).astype(bf16)
-            grad_projected[rows, at_value] = jnp.where(left, *to_value).astype(bf16)
-            return carry
-
-        lax.fori_loop(0, HEADS // 4, pair_step, 0)
+                to_query[block].append(dot(grad16, projected[rows, at_key], NN))
+                to_key[block].append(dot(grad16, projected[rows, at_query], TN))
+                both = both + grad16.astype(f32)
+            total = jnp.zeros((8, 512), f32)
+            blank = jnp.zeros((8, 256), f32)
+            for g in range(32):
+                lines = jnp.concatenate([both[8 * g : 8 * g + 8], blank], axis=1)
+                total = total + pltpu.roll(lines, 255 - 8 * g, 1)
+            diagonals[first_head + 2 * pair + side] = total
+        for block, rows in enumerate(blocks):
+            grad_projected[rows, at_query] = (
+                score_scale * jnp.where(left, *to_query[block])
+            ).astype(bf16)
+            grad_projected[rows, at_key] = (
+                score_scale * jnp.where(left, *to_key[block])
+            ).astype(bf16)
+            grad_projected[rows, at_value] = jnp.where(left, *to_value[block]).astype(bf16)
+        return carry
+
+    lax.fori_loop(0, HEADS // 4, pair_step, 0)
 
 
 def weights_backward(x_own, x_other, attn_in, grad_projected, weights, diagonals, keep, got, *refs):
@@ -514,8 +531,8 @@
     whole[:, QKV + HALF :] = jnp.where(tall == AT_ATTN, sums, extra).astype(bf16)
 
 
-def input_backward(x_ref, grad_after, to_own, got, weights, grad_in):
-    gain = gain_row(weights[:, QKV:], AT_ATTN)
+def input_backward(x_ref, grad_after, to_own, got, extras, grad_in):
+    gain = gain_row(extras[...], AT_ATTN)
     back, _ = norm_backward(x_ref[...].astype(f32), to_own[...] + got[...], gain)
     grad_in[...] = grad_after[...] + back
 
@@ -565,12 +582,12 @@
     def over_exp(value):
         return lax.all_to_all(value, "exp", split_axis=0, concat_axis=0, tiled=True)
 
-    def over_groups(value):
-        return lax.all_gather(value, "rep", axis=0, tiled=True)
-
-    packed, beside = call(
+    def over_groups(value, step):
+        return lax.ppermute(value, "rep", z_shift(step))
+
+    (packed,) = call(
         pack_weights,
-        [((EXPERTS, 24, WIDE1), bf16), ((24, WIDE2), bf16)],
+        [((EXPERTS, 24, SENT), bf16)],
         w_query,
         w_key,
         w_value,
@@ -581,8 +598,7 @@
         rel_bias,
         smem=0,
     )
-    weights2 = lax.all_gather(beside, "exp", axis=0, tiled=True)
-    weights1 = over_exp(packed).reshape(D, WIDE1)
+    weights1 = over_exp(packed).reshape(D, SENT)
     x_other = on_exp(hidden_in, SWAP)
     doc_row = jnp.stack([doc_ids, on_exp(doc_ids, SWAP)])
     doc_col = doc_row.reshape(2 * TOK, 1)
@@ -603,9 +619,11 @@
 
     slot_mix = exchange(hold_until(placed_grads, weights1))
 
-    attn_in, projected, probs, att_own, att_send = call(
+    extras, out_half, attn_in, projected, probs, att_own, att_send = call(
         attention_forward,
         [
+            ((D, 128), bf16),
+            ((D, HALF), bf16),
             ((2 * TOK, D), bf16),
             ((2 * TOK, QKV), bf16),
             ((HEADS, TOK, TOK), bf16),
@@ -623,9 +641,11 @@
         bytes_accessed=10_000_000,
     )
     att_other = on_exp(att_send, SWAP)
-    after, ffn_in, router, gate, outbound = call(
+    out_got = on_exp(out_half, SWAP)
+    weights2, after, ffn_in, router, gate, outbound = call(
         route_forward,
         [
+            ((D, D), bf16),
             ((TOK, D), f32),
             ((TOK, D), bf16),
             ((TOK, 128), f32),
@@ -638,14 +658,17 @@
         att_own,
         att_other,
         placer,
-        weights2,
+        out_half,
+        out_got,
+        extras,
+        after=[slot_mix],
         flops=3_000_000_000,
         bytes_accessed=8_000_000,
     )
+    mix1, mix3 = over_groups(slot_mix, 1), over_groups(slot_mix, 3)
     slot_rows = exchange(outbound)
-    all_mix = over_groups(hold_until(slot_mix, att_send))
-    all_rows = over_groups(slot_rows)
-    produced, back = run_expert(slot_rows, slot_mix, w_in, w_down)
+    rows1, rows3 = over_groups(slot_rows, 1), over_groups(slot_rows, 3)
+    produced, back = run_expert(slot_rows, slot_mix, w_in, w_down, [mix1, mix3])
     grad_back = exchange(back)
     returned = exchange(produced)
 
@@ -670,7 +693,9 @@
         placer,
         grad_back,
         weights2,
+        extras,
         scratch=[pltpu.VMEM((D, D), bf16)],
+        after=[rows1, rows3],
         flops=4_000_000_000,
         bytes_accessed=10_000_000,
     )
@@ -687,17 +712,6 @@
         flops=9_000_000_000,
         bytes_accessed=8_000_000,
     )
-    (block_out,) = call(
-        mix_out,
-        [((TOK, D), bf16)],
-        after,
-        gate,
-        placer,
-        returned,
-        smem=0,
-        flops=200_000_000,
-        bytes_accessed=3_000_000,
-    )
     whole, to_own, to_send = call(
         weights_backward,
         [((D, SENT), bf16), ((TOK, D), f32), ((TOK, D), f32)],
@@ -710,13 +724,20 @@
         keep,
         got,
         smem=0,
-        after=[block_out],
         flops=5_000_000_000,
         bytes_accessed=10_000_000,
     )
-    parts = over_exp(whole.reshape(EXPERTS, 24, SENT))
+    parts = over_exp(hold_until(whole, returned).reshape(EXPERTS, 24, SENT))
     to_got = on_exp(to_send, SWAP)
-    grad_w_in, grad_w_down = run_expert_weights(group, all_rows, all_mix, w_in, w_down, to_send)
+    kept = run_expert_weights(
+        group,
+        [slot_rows, rows1, rows3],
+        [slot_mix, mix1, mix3],
+        w_in,
+        w_down,
+        [],
+        to_send,
+    )
     (grad_in,) = call(
         input_backward,
         [((TOK, D), f32)],
@@ -724,13 +745,34 @@
         grad_after,
         to_own,
         to_got,
-        weights1,
+        extras,
         smem=0,
         flops=10_000_000,
         bytes_accessed=5_000_000,
     )
+    (block_out,) = call(
+        mix_out,
+        [((TOK, D), bf16)],
+        after,
+        gate,
+        placer,
+        returned,
+        smem=0,
+        after=[to_send],
+        flops=200_000_000,
+        bytes_accessed=3_000_000,
+    )
     (own,) = call(
-        sum_parts, [((24, 2 * SENT), bf16)], parts, smem=0, after=[grad_w_in, grad_in]
+        sum_parts, [((24, 2 * SENT), bf16)], parts, smem=0, after=[*kept, grad_in, block_out]
+    )
+    grad_w_in, grad_w_down = run_expert_weights(
+        group,
+        [over_groups(slot_rows, 2)],
+        [over_groups(slot_mix, 2)],
+        w_in,
+        w_down,
+        kept,
+        own,
     )
     others = [lax.ppermute(own, "rep", z_shift(k)) for k in (1, 2, 3)]
     (
@@ -749,6 +791,7 @@
         own,
         *others,
         smem=0,
+        after=[grad_w_in, grad_w_down],
     )
     return (
         block_out,

time: 247 us -> 237 us (0.960)
  starting transfers between devices: 25.5 us -> 48.9 us
  blocking collectives: 40.7 us -> 23.4 us
  between operations: 13.9 us -> 0.84 us
  waiting for transfers between devices: 63.6 us -> 57.6 us
  local copies, waits for them, and re-layouts: 9.29 us -> 11.8 us
    all_to_all x4 -> x5, waiting for transfers between devices: 29.5 us -> 52.9 us  [over_exp(): return lax.all_to_all(value, 'exp', split_axis=0, concat_axis=0, tiled=True)]
    all_gather x3 -> x0, waiting for transfers between devices: 21.6 us -> none  [the longest x2 12.5 us: over_groups(): return lax.all_gather(value, 'rep', axis=0, tiled=True)]
    all_to_all x2 -> x1, blocking collectives: 40.7 us -> 23.4 us  [over_exp(): return lax.all_to_all(value, 'exp', split_axis=0, concat_axis=0, tiled=True)]
    ppermute x0 -> x6, starting transfers between devices: none -> 11.8 us  [over_groups(): return lax.ppermute(value, 'rep', z_shift(step))]
    all_to_all x4 -> x5, starting transfers between devices: 19.5 us -> 30.2 us  [over_exp(): return lax.all_to_all(value, 'exp', split_axis=0, concat_axis=0, tiled=True)]
    ppermute x3, waiting for transfers between devices: 6.65 us -> 0.01 us  [on_device(): others = [lax.ppermute(own, 'rep', z_shift(k)) for k in (1, 2, 3)]]
    pallas_call x2 -> x3, Pallas kernels: 35.8 us -> 38.7 us  [the longest x2 22 us: run_expert_weights(): pl.pallas_call(run, grid_spec=pltpu.PrefetchScalarGridSpec(num_scalar_pre...]
    pallas_call x11, Pallas kernels: 56.2 us -> 53.4 us  [call(): pl.pallas_call(run, out_shape=[jax.ShapeDtypeStruct(shape, kind) for shap...]
  transfers between devices with their start and end apart: 16 -> 21, of which waited for: 8 -> 6; matrix products, arithmetic and copies ran while one was open for 1% -> 1% of each run, Pallas kernels for 27% -> 33%
where the time goes in v1:
time: 237 us; the launch traced here: 236 us
  Pallas kernels  92 us (39%)
  waiting for transfers between devices  57.6 us (24%)
  starting transfers between devices  48.9 us (21%)
  blocking collectives  23.4 us (10%)
  local copies, waits for them, and re-layouts  11.8 us (5%)
    pallas_call x11, Pallas kernels, call(): pl.pallas_call(run, out_shape=[jax.ShapeDtypeStruct(shape, kind) for shap...  53.4 us
    all_to_all x5, waiting for transfers between devices, over_exp(): return lax.all_to_all(value, 'exp', split_axis=0, concat_axis=0, tiled=True)  52.9 us
    all_to_all x5, starting transfers between devices, over_exp(): return lax.all_to_all(value, 'exp', split_axis=0, concat_axis=0, tiled=True)  30.2 us
    all_to_all x1, blocking collectives, over_exp(): return lax.all_to_all(value, 'exp', split_axis=0, concat_axis=0, tiled=True)  23.4 us
    pallas_call x2, Pallas kernels, run_expert_weights(): pl.pallas_call(run, grid_spec=pltpu.PrefetchScalarGridSpec(num_scalar_pre...  22 us
    pallas_call x1, Pallas kernels, run_expert(): pl.pallas_call(run, grid=(FF // BLOCK,), in_specs=[wide, whole, pl.BlockS...  16.6 us
    ppermute x6, starting transfers between devices, over_groups(): return lax.ppermute(value, 'rep', z_shift(step))  11.8 us
    unnamed x43, local copies, waits for them, and re-layouts  11.8 us
  transfers between devices with their start and end apart: 21, of which 6 were waited for; matrix products, arithmetic and copies ran while one was open for 1% of the time, Pallas kernels for 33%

profile of v1, /device:TPU:0, one launch (start us, length us, event | category | flops | bytes accessed | tf_op | source)
XLA Modules:
  0.0 235.8 jit_solution(14350516252673787372)
XLA Ops:
  3.2 7.5 %all-to-all-start = ((bf16[32,24,1664]{2,1,0:T(8,128)(2,1)}), bf16[32,24,1664]{2,1,0:T(8,128)(2,1)S(1)}, u32[]{:S(2)}, u32[]{:S(2)}) async-start(bf16[32,24,1664]{2,1,0:T(8,128)(2,1)} %shard_map.229), calls=%async_computation | async-start | bytes 5111808 | tf_op jit(solution)/shard_map/all_to_all | solution.py:583
  12.7 2.8 %shard_map.231 = (bf16[256,512]{1,0:T(8,128)(2,1)}, bf16[512,768]{1,0:T(8,128)(2,1)}) custom-call(s32[256,1]{1,0:T(8,128)} %copy.32.refs_0_.refs_2_.refs_1_, bf16[256,768]{1,0:T(8,128)(2,1)} %refs_2_.7), custom_call_target="tpu_custom_call" | custom-call | flops 500000000 | bytes 2000000 | tf_op jit(solution)/shard_map/pallas_call | solution.py:66
  17.0 29.1 %all-to-all-done = bf16[32,24,1664]{2,1,0:T(8,128)(2,1)S(1)} async-done(((bf16[32,24,1664]{2,1,0:T(8,128)(2,1)}), bf16[32,24,1664]{2,1,0:T(8,128)(2,1)S(1)}, u32[]{:S(2)}, u32[]{:S(2)}) %all-to-all-start) | async-done | bytes 2555936 | tf_op jit(solution)/shard_map/all_to_all | solution.py:583
  47.5 3.9 %all-to-all-start.1 = ((bf16[32,16,768]{2,1,0:T(8,128)(2,1)}), bf16[32,16,768]{2,1,0:T(8,128)(2,1)S(1)}, u32[]{:S(2)}, u32[]{:S(2)}) async-start(bf16[32,16,768]{2,1,0:T(8,128)(2,1)} %bitcast.31), calls=%async_computation.1 | async-start | bytes 1572864 | tf_op jit(solution)/shard_map/all_to_all | solution.py:583
  52.2 11.7 %shard_map.230 = (bf16[768,128]{1,0:T(8,128)(2,1)}, bf16[768,384]{1,0:T(8,128)(2,1)}, bf16[512,768]{1,0:T(8,128)(2,1)}, bf16[512,1152]{1,0:T(8,128)(2,1)}, bf16[...) custom-call(s32[3]{0:T(128)} %pad_add_fusion.1.refs_0_, bf16[256,768]{1,0:T(8,128)(2,1)} %refs_0_.6, ...), custom_call_target="tpu_custom_call" | custom-call | flops 8999999488 | bytes 10000000 | tf_op jit(solution)/shard_map/pallas_call | solution.py:66
  67.6 4.4 %shard_map.233 = (bf16[768,768]{1,0:T(8,128)(2,1)}, f32[256,768]{1,0:T(8,128)}, bf16[256,768]{1,0:T(8,128)(2,1)}, f32[256,128]{1,0:T(8,128)}, f32[256,1]{1,0:T(8,128)}, /*index=5*/bf16[512,896]{1,0:T(8,128)(2,1)}) custom-call(s32[3]{0:T(128)} %pad_add_fusion.1.refs_0_, bf16[256,768]{1,0:T(8,128)(2,1)} %refs_0_.6, s32[256,1]{1,0:T(8,128)} %copy.32.refs_0_.refs_2_.refs_1_, ...), custom_call_target="tpu_custom_call" | custom-call | flops 3000000000 | bytes 8000000 | tf_op jit(solution)/shard_map/pallas_call | solution.py:66
  72.0 7.4 %all-to-all-start.2 = ((bf16[32,16,896]{2,1,0:T(8,128)(2,1)}), bf16[32,16,896]{2,1,0:T(8,128)(2,1)S(1)}, u32[]{:S(2)}, u32[]{:S(2)}) async-start(bf16[32,16,896]{2,1,0:T(8,128)(2,1)} %bitcast.37), calls=%async_computation.2 | async-start | bytes 1835008 | tf_op jit(solution)/shard_map/all_to_all | solution.py:583
  83.6 11.7 %all-to-all-done.2 = bf16[32,16,896]{2,1,0:T(8,128)(2,1)S(1)} async-done(((bf16[32,16,896]{2,1,0:T(8,128)(2,1)}), bf16[32,16,896]{2,1,0:T(8,128)(2,1)S(1)}, u32[]{:S(2)}, u32[]{:S(2)}) %all-to-all-start.2) | async-done | bytes 917536 | tf_op jit(solution)/shard_map/all_to_all | solution.py:583
  99.4 2.7 %collective-permute-done.4.refs_4_ = bf16[512,768]{1,0:T(8,128)(2,1)S(1)} collective-permute-done((bf16[512,768]{1,0:T(8,128)(2,1)}, bf16[512,768]{1,0:T(8,128)(2,1)S(1)}, u32[]{:S(2)}, u32[]{:S(2)}) %collective-permute-start.4) | collective-permute-done | bytes 786464 | tf_op jit(solution)/shard_map/ppermute | solution.py:586
  102.9 16.6 %shard_map.234 = (bf16[512,768]{1,0:T(8,128)(2,1)}, bf16[512,896]{1,0:T(8,128)(2,1)}) custom-call(bf16[512,896]{1,0:T(8,128)(2,1)} %bitcast.34, bf16[512,768]{1,0:T(8,128)(2,1)} %bitcast.43, bf16[1,768,3072]{2,1,0:T(8,128)(2,1)} %refs_2_.8, bf16[1,3072,768]{2,1,0:T(8,128)(2,1)} %refs_3_.5, bf16[512,768]{1,0:T(8,128)(2,1)} %copy-done.14, ...), custom_call_target="tpu_custom_call" | custom-call | flops 9663676416 | bytes 14680064 | tf_op jit(solution)/shard_map/pallas_call | solution.py:350
  119.6 23.4 %all_to_all.30 = bf16[32,16,896]{2,1,0:T(8,128)(2,1)} all-to-all(bf16[32,16,896]{2,1,0:T(8,128)(2,1)} %bitcast.39), channel_id=1, replica_groups=mesh['rep'=4,'exp'=32] {'exp'}, dimensions={0} | all-to-all | bytes 1835008 | tf_op jit(solution)/shard_map/all_to_all | solution.py:583
  144.3 6.0 %shard_map.235 = (f32[256,768]{1,0:T(8,128)}, bf16[256,384]{1,0:T(8,128)(2,1)}, bf16[256,384]{1,0:T(8,128)(2,1)}, bf16[768,512]{1,0:T(8,128)(2,1)}, bf16[768,384]{1,0:T(8,128)(2,1)}) custom-call(s32[3]{0:T(128)} %pad_add_fusion.1.refs_0_, s32[256,1]{1,0:T(8,128)} %copy.32.refs_0_.refs_2_.refs_1_, bf16[256,768]{1,0:T(8,128)(2,1)} %refs_2_.7, ...), custom_call_target="tpu_custom_call" | custom-call | flops 4000000000 | bytes 10000000 | tf_op jit(solution)/shard_map/pallas_call | solution.py:66
  150.4 3.9 %all-to-all-start.3 = ((bf16[32,16,768]{2,1,0:T(8,128)(2,1)}), bf16[32,16,768]{2,1,0:T(8,128)(2,1)S(1)}, u32[]{:S(2)}, u32[]{:S(2)}) async-start(bf16[32,16,768]{2,1,0:T(8,128)(2,1)} %bitcast.12), calls=%async_computation.3 | async-start | bytes 1572864 | tf_op jit(solution)/shard_map/all_to_all | solution.py:583
  155.3 7.2 %shard_map.236 = (bf16[512,1152]{1,0:T(8,128)(2,1)}, f32[16,8,512]{2,1,0:T(8,128)}) custom-call(s32[3]{0:T(128)} %pad_add_fusion.1.refs_0_, bf16[512,1152]{1,0:T(8,128)(2,1)} %get-tuple-element.62.refs_1_, bf16[12,256,256]{2,1,0:T(8,128)(2,1)} %get-tuple-element.63.refs_2_, bf16[256,384]{1,0:T(8,128)(2,1)} %get-tuple-element.68.refs_3_, ...), custom_call_target="tpu_custom_call" | custom-call | flops 8999999488 | bytes 8000000 | tf_op jit(solution)/shard_map/pallas_call | solution.py:66
  163.4 8.4 %shard_map.237 = (bf16[768,1664]{1,0:T(8,128)(2,1)}, f32[256,768]{1,0:T(8,128)}, f32[256,768]{1,0:T(8,128)}) custom-call(bf16[256,768]{1,0:T(8,128)(2,1)} %refs_0_.6, bf16[256,768]{1,0:T(8,128)(2,1)} %copy-done.17, bf16[512,768]{1,0:T(8,128)(2,1)} %get-tuple-element.61.refs_2_, bf16[512,1152]{1,0:T(8,128)(2,1)} %get-tuple-element.70.refs_3_, ...), custom_call_target="tpu_custom_call" | custom-call | flops 5000000000 | bytes 10000000 | tf_op jit(solution)/shard_map/pallas_call | solution.py:66
  172.7 7.5 %all-to-all-start.5 = ((bf16[32,24,1664]{2,1,0:T(8,128)(2,1)}), bf16[32,24,1664]{2,1,0:T(8,128)(2,1)S(1)}, u32[]{:S(2)}, u32[]{:S(2)}) async-start(bf16[32,24,1664]{2,1,0:T(8,128)(2,1)} %bitcast.28), calls=%async_computation.5 | async-start | bytes 5111808 | tf_op jit(solution)/shard_map/all_to_all | solution.py:583
  180.2 2.8 %collective-permute-start.14 = (bf16[512,896]{1,0:T(8,128)(2,1)S(1)}, bf16[512,896]{1,0:T(8,128)(2,1)}, u32[]{:S(2)}, u32[]{:S(2)}) collective-permute-start(bf16[512,896]{1,0:T(8,128)(2,1)S(1)} %bitcast.36), channel_id=1, source_target_pairs={{0,64},{32,96},{64,0},{96,32},{1,65},{33,97},{65,1},{97,33},{2,66}... | collective-permute-start | bytes 2752520 | tf_op jit(solution)/shard_map/ppermute | solution.py:586
  183.8 2.6 %shard_map.238.refs_4_ = bf16[256,768]{1,0:T(8,128)(2,1)} custom-call(f32[256,768]{1,0:T(8,128)} %get-tuple-element.57.refs_5_.refs_0_, f32[256,1]{1,0:T(8,128)} %get-tuple-element.58.refs_8_.refs_1_, bf16[256,512]{1,0:T(8,128)(2,1)} %get-tuple-element.53.refs_5_.refs_9_.refs_2_, bf16[512,768]{1,0:T(8,128)(2,1)} %bitcast.30, ...), custom_call_target="tpu_custom_call" | custom-call | flops 200000000 | bytes 3000000 | tf_op jit(solution)/shard_map/pallas_call | solution.py:66
  186.4 13.9 %shard_map.241 = (f32[1,768,768]{2,1,0:T(8,128)}, f32[1,768,768]{2,1,0:T(8,128)}) custom-call(s32[1]{0:T(128)} %bitcast.17.pos, bf16[512,896]{1,0:T(8,128)(2,1)} %bitcast.35, bf16[512,896]{1,0:T(8,128)(2,1)} %copy-done.12, bf16[512,896]{1,0:T(8,128)(2,1)} %copy-done.13, bf16[512,768]{1,0:T(8,128)(2,1)} %bitcast.45, bf16[512,768]{1,0:T(8,128)(2,1)} %copy-done.14, ...), custom_call_target="tpu_custom_call" | custom-call | flops 7247757312 | bytes 14680064 | tf_op jit(solution)/shard_map/pallas_call | solution.py:385
  200.4 3.0 %shard_map.239.refs_3_ = f32[256,768]{1,0:T(8,128)} custom-call(bf16[256,768]{1,0:T(8,128)(2,1)} %refs_0_.6, f32[256,768]{1,0:T(8,128)} %get-tuple-element.75.refs_1_, f32[256,768]{1,0:T(8,128)} %get-tuple-element.76.refs_2_, f32[256,768]{1,0:T(8,128)} %collective-permute-done.10.refs_3_, bf16[768,128]{1,0:T(8,128)(2,1)} %get-tuple-element.55.refs_8_.refs_12_.refs_4_), custom_call_target="tpu_custom_call" | custom-call | flops 10000000 | bytes 5000000 | tf_op jit(solution)/shard_map/pallas_call | solution.py:66
  203.4 12.1 %all-to-all-done.5.refs_0_ = bf16[32,24,1664]{2,1,0:T(8,128)(2,1)S(1)} async-done(((bf16[32,24,1664]{2,1,0:T(8,128)(2,1)}), bf16[32,24,1664]{2,1,0:T(8,128)(2,1)S(1)}, u32[]{:S(2)}, u32[]{:S(2)}) %all-to-all-start.5) | async-done | bytes 2555936 | tf_op jit(solution)/shard_map/all_to_all | solution.py:583
  217.0 2.7 %shard_map.242.refs_6_.refs_0_ = bf16[24,3328]{1,0:T(8,128)(2,1)} custom-call(bf16[32,24,1664]{2,1,0:T(8,128)(2,1)} %copy-done, f32[1,768,768]{2,1,0:T(8,128)} %get-tuple-element.78.refs_1_.refs_4_, f32[1,768,768]{2,1,0:T(8,128)} %get-tuple-element.79.refs_2_.refs_5_, f32[256,768]{1,0:T(8,128)} %shard_map.239.refs_3_, bf16[256,768]{1,0:T(8,128)(2,1)} %shard_map.238.refs_4_), custom_call_target="tpu_custom_call" | custom-call | tf_op jit(solution)/shard_map/pallas_call | solution.py:66
  220.8 2.9 %collective-permute-start.12 = (bf16[24,3328]{1,0:T(8,128)(2,1)}, bf16[24,3328]{1,0:T(8,128)(2,1)S(1)}, u32[]{:S(2)}, u32[]{:S(2)}) collective-permute-start(bf16[24,3328]{1,0:T(8,128)(2,1)} %shard_map.242.refs_6_.refs_0_), channel_id=1, source_target_pairs={{0,64},{32,96},{64,0},{96,32},{1,65},{33,97},{65,1},{97,33},{2,66}... | collective-permute-start | bytes 479240 | tf_op jit(solution)/shard_map/ppermute | solution.py:777
  225.1 8.1 %shard_map.243 = (f32[1,768,768]{2,1,0:T(8,128)}, f32[1,768,768]{2,1,0:T(8,128)}) custom-call(s32[1]{0:T(128)} %bitcast.17.pos, bf16[512,896]{1,0:T(8,128)(2,1)} %collective-permute-done.14.refs_0_, bf16[512,768]{1,0:T(8,128)(2,1)} %collective-permute-done.15.refs_1_, bf16[1,768,3072]{2,1,0:T(8,128)(2,1)} %refs_2_.8, ...), custom_call_target="tpu_custom_call", output_to_operand_aliasing={{0}: (5, {}), {1}: (6, {})} | custom-call | flops 2415919104 | bytes 14680064 | tf_op jit(solution)/shard_map/pallas_call | solution.py:385
  (80 shorter events, 32.4 us)
Async XLA Ops:
  3.2 7.6 %copy-start.6 = (bf16[256,768]{1,0:T(8,128)(2,1)S(1)}, bf16[256,768]{1,0:T(8,128)(2,1)}, u32[]{:S(2)}) copy-start(bf16[256,768]{1,0:T(8,128)(2,1)} %refs_0_.6) | copy-start | bytes 1179652
  3.2 7.9 %copy-start.11 = (s32[256]{0:T(256)S(1)}, s32[256]{0:T(256)}, u32[]{:S(2)}) copy-start(s32[256]{0:T(256)} %param.15) | copy-start | bytes 3076
  3.2 8.2 %copy-start.10 = (s32[256,1]{0,1:T(1,128)S(1)}, s32[256,1]{0,1:T(1,128)}, u32[]{:S(2)}) copy-start(s32[256,1]{0,1:T(1,128)} %param.16) | copy-start | bytes 3076
  3.2 42.9 %all-to-all-start = ((bf16[32,24,1664]{2,1,0:T(8,128)(2,1)}), bf16[32,24,1664]{2,1,0:T(8,128)(2,1)S(1)}, u32[]{:S(2)}, u32[]{:S(2)}) async-start(bf16[32,24,1664]{2,1,0:T(8,128)(2,1)} %shard_map.229), calls=%async_computation | async-start | bytes 5111808 | tf_op jit(solution)/shard_map/all_to_all | solution.py:583
  10.7 40.7 %collective-permute-start = (bf16[256,768]{1,0:T(8,128)(2,1)S(1)}, bf16[256,768]{1,0:T(8,128)(2,1)S(1)}, u32[]{:S(2)}, u32[]{:S(2)}) collective-permute-start(bf16[256,768]{1,0:T(8,128)(2,1)S(1)} %copy-done.6), channel_id=1, source_target_pairs={{0,1},{1,0},{2,3},{3,2},{4,5},{5,4},{6,7},{7,6},{8,9},{9,8},{10,11... | collective-permute-start | bytes 1179656 | tf_op jit(solution)/shard_map/ppermute | solution.py:46
  11.1 4.4 %collective-permute-start.1 = (s32[256]{0:T(256)S(1)}, s32[256]{0:T(256)S(1)}, u32[]{:S(2)}, u32[]{:S(2)}) collective-permute-start(s32[256]{0:T(256)S(1)} %copy-done.11), channel_id=1, source_target_pairs={{0,1},{1,0},{2,3},{3,2},{4,5},{5,4},{6,7},{7,6},{8,9},{9,8},{10,11... | collective-permute-start | bytes 3080 | tf_op jit(solution)/shard_map/ppermute | solution.py:46
  47.5 18.9 %all-to-all-start.1 = ((bf16[32,16,768]{2,1,0:T(8,128)(2,1)}), bf16[32,16,768]{2,1,0:T(8,128)(2,1)S(1)}, u32[]{:S(2)}, u32[]{:S(2)}) async-start(bf16[32,16,768]{2,1,0:T(8,128)(2,1)} %bitcast.31), calls=%async_computation.1 | async-start | bytes 1572864 | tf_op jit(solution)/shard_map/all_to_all | solution.py:583
  63.9 2.5 %collective-permute-start.3 = (bf16[768,384]{1,0:T(8,128)(2,1)}, bf16[768,384]{1,0:T(8,128)(2,1)S(1)}, u32[]{:S(2)}, u32[]{:S(2)}) collective-permute-start(bf16[768,384]{1,0:T(8,128)(2,1)} %get-tuple-element.54.refs_6_), channel_id=1, source_target_pairs={{0,1},{1,0},{2,3},{3,2},{4,5},{5,4},{6,7},{7,6},{8,9},{9,8},{10,11... | collective-permute-start | bytes 1769480 | tf_op jit(solution)/shard_map/ppermute | solution.py:46
  64.1 2.3 collective-permute-start.2
  72.0 23.3 %all-to-all-start.2 = ((bf16[32,16,896]{2,1,0:T(8,128)(2,1)}), bf16[32,16,896]{2,1,0:T(8,128)(2,1)S(1)}, u32[]{:S(2)}, u32[]{:S(2)}) async-start(bf16[32,16,896]{2,1,0:T(8,128)(2,1)} %bitcast.37), calls=%async_computation.2 | async-start | bytes 1835008 | tf_op jit(solution)/shard_map/all_to_all | solution.py:583
  79.4 22.6 %collective-permute-start.4 = (bf16[512,768]{1,0:T(8,128)(2,1)}, bf16[512,768]{1,0:T(8,128)(2,1)S(1)}, u32[]{:S(2)}, u32[]{:S(2)}) collective-permute-start(bf16[512,768]{1,0:T(8,128)(2,1)} %bitcast.41), channel_id=1, source_target_pairs={{0,32},{32,64},{64,96},{96,0},{1,33},{33,65},{65,97},{97,1},{2,34}... | collective-permute-start | bytes 2359304 | tf_op jit(solution)/shard_map/ppermute | solution.py:586
  81.4 20.7 %collective-permute-start.5 = (bf16[512,768]{1,0:T(8,128)(2,1)}, bf16[512,768]{1,0:T(8,128)(2,1)}, u32[]{:S(2)}, u32[]{:S(2)}) collective-permute-start(bf16[512,768]{1,0:T(8,128)(2,1)} %bitcast.42), channel_id=1, source_target_pairs={{0,96},{32,0},{64,32},{96,64},{1,97},{33,1},{65,33},{97,65},{2,98}... | collective-permute-start | bytes 2359304 | tf_op jit(solution)/shard_map/ppermute | solution.py:586
  95.3 47.7 %collective-permute-start.6 = (bf16[512,896]{1,0:T(8,128)(2,1)S(1)}, bf16[512,896]{1,0:T(8,128)(2,1)S(1)}, u32[]{:S(2)}, u32[]{:S(2)}) collective-permute-start(bf16[512,896]{1,0:T(8,128)(2,1)S(1)} %bitcast.32), channel_id=1, source_target_pairs={{0,32},{32,64},{64,96},{96,0},{1,33},{33,65},{65,97},{97,1},{2,34}... | collective-permute-start | bytes 2752520 | tf_op jit(solution)/shard_map/ppermute | solution.py:586
  97.2 45.8 %collective-permute-start.7 = (bf16[512,896]{1,0:T(8,128)(2,1)S(1)}, bf16[512,896]{1,0:T(8,128)(2,1)S(1)}, u32[]{:S(2)}, u32[]{:S(2)}) collective-permute-start(bf16[512,896]{1,0:T(8,128)(2,1)S(1)} %bitcast.33), channel_id=1, source_target_pairs={{0,96},{32,0},{64,32},{96,64},{1,97},{33,1},{65,33},{97,65},{2,98}... | collective-permute-start | bytes 2752520 | tf_op jit(solution)/shard_map/ppermute | solution.py:586
  150.3 4.3 %collective-permute-start.8 = (bf16[256,384]{1,0:T(8,128)(2,1)}, bf16[256,384]{1,0:T(8,128)(2,1)S(1)}, u32[]{:S(2)}, u32[]{:S(2)}) collective-permute-start(bf16[256,384]{1,0:T(8,128)(2,1)} %get-tuple-element.69), channel_id=1, source_target_pairs={{0,1},{1,0},{2,3},{3,2},{4,5},{5,4},{6,7},{7,6},{8,9},{9,8},{10,11... | collective-permute-start | bytes 589832 | tf_op jit(solution)/shard_map/ppermute | solution.py:46
  150.4 21.4 %all-to-all-start.3 = ((bf16[32,16,768]{2,1,0:T(8,128)(2,1)}), bf16[32,16,768]{2,1,0:T(8,128)(2,1)S(1)}, u32[]{:S(2)}, u32[]{:S(2)}) async-start(bf16[32,16,768]{2,1,0:T(8,128)(2,1)} %bitcast.12), calls=%async_computation.3 | async-start | bytes 1572864 | tf_op jit(solution)/shard_map/all_to_all | solution.py:583
  154.3 8.2 %collective-permute-start.9 = (bf16[768,384]{1,0:T(8,128)(2,1)}, bf16[768,384]{1,0:T(8,128)(2,1)S(1)}, u32[]{:S(2)}, u32[]{:S(2)}) collective-permute-start(bf16[768,384]{1,0:T(8,128)(2,1)} %get-tuple-element.73), channel_id=1, source_target_pairs={{0,1},{1,0},{2,3},{3,2},{4,5},{5,4},{6,7},{7,6},{8,9},{9,8},{10,11... | collective-permute-start | bytes 1769480 | tf_op jit(solution)/shard_map/ppermute | solution.py:46
  172.7 42.8 %all-to-all-start.5 = ((bf16[32,24,1664]{2,1,0:T(8,128)(2,1)}), bf16[32,24,1664]{2,1,0:T(8,128)(2,1)S(1)}, u32[]{:S(2)}, u32[]{:S(2)}) async-start(bf16[32,24,1664]{2,1,0:T(8,128)(2,1)} %bitcast.28), calls=%async_computation.5 | async-start | bytes 5111808 | tf_op jit(solution)/shard_map/all_to_all | solution.py:583
  180.2 44.9 %collective-permute-start.14 = (bf16[512,896]{1,0:T(8,128)(2,1)S(1)}, bf16[512,896]{1,0:T(8,128)(2,1)}, u32[]{:S(2)}, u32[]{:S(2)}) collective-permute-start(bf16[512,896]{1,0:T(8,128)(2,1)S(1)} %bitcast.36), channel_id=1, source_target_pairs={{0,64},{32,96},{64,0},{96,32},{1,65},{33,97},{65,1},{97,33},{2,66}... | collective-permute-start | bytes 2752520 | tf_op jit(solution)/shard_map/ppermute | solution.py:586
  183.0 17.4 %collective-permute-start.10 = (f32[256,768]{1,0:T(8,128)}, f32[256,768]{1,0:T(8,128)}, u32[]{:S(2)}, u32[]{:S(2)}) collective-permute-start(f32[256,768]{1,0:T(8,128)} %get-tuple-element.74.refs_4_.refs_8_), channel_id=1, source_target_pairs={{0,1},{1,0},{2,3},{3,2},{4,5},{5,4},{6,7},{7,6},{8,9},{9,8},{10,11... | collective-permute-start | bytes 2359304 | tf_op jit(solution)/shard_map/ppermute | solution.py:46
  183.0 42.1 %collective-permute-start.15 = (bf16[512,768]{1,0:T(8,128)(2,1)}, bf16[512,768]{1,0:T(8,128)(2,1)}, u32[]{:S(2)}, u32[]{:S(2)}) collective-permute-start(bf16[512,768]{1,0:T(8,128)(2,1)} %bitcast.44), channel_id=1, source_target_pairs={{0,64},{32,96},{64,0},{96,32},{1,65},{33,97},{65,1},{97,33},{2,66}... | collective-permute-start | bytes 2359304 | tf_op jit(solution)/shard_map/ppermute | solution.py:586
  219.7 13.5 %collective-permute-start.11 = (bf16[24,3328]{1,0:T(8,128)(2,1)}, bf16[24,3328]{1,0:T(8,128)(2,1)S(1)}, u32[]{:S(2)}, u32[]{:S(2)}) collective-permute-start(bf16[24,3328]{1,0:T(8,128)(2,1)} %shard_map.242.refs_6_.refs_0_), channel_id=1, source_target_pairs={{0,32},{32,64},{64,96},{96,0},{1,33},{33,65},{65,97},{97,1},{2,34}... | collective-permute-start | bytes 479240 | tf_op jit(solution)/shard_map/ppermute | solution.py:777
  220.8 12.4 %collective-permute-start.12 = (bf16[24,3328]{1,0:T(8,128)(2,1)}, bf16[24,3328]{1,0:T(8,128)(2,1)S(1)}, u32[]{:S(2)}, u32[]{:S(2)}) collective-permute-start(bf16[24,3328]{1,0:T(8,128)(2,1)} %shard_map.242.refs_6_.refs_0_), channel_id=1, source_target_pairs={{0,64},{32,96},{64,0},{96,32},{1,65},{33,97},{65,1},{97,33},{2,66}... | collective-permute-start | bytes 479240 | tf_op jit(solution)/shard_map/ppermute | solution.py:777
  223.7 9.5 %collective-permute-start.13 = (bf16[24,3328]{1,0:T(8,128)(2,1)}, bf16[24,3328]{1,0:T(8,128)(2,1)S(1)}, u32[]{:S(2)}, u32[]{:S(2)}) collective-permute-start(bf16[24,3328]{1,0:T(8,128)(2,1)} %shard_map.242.refs_6_.refs_0_), channel_id=1, source_target_pairs={{0,96},{32,0},{64,32},{96,64},{1,97},{33,1},{65,33},{97,65},{2,98}... | collective-permute-start | bytes 479240 | tf_op jit(solution)/shard_map/ppermute | solution.py:777
  (17 other events, 28.4 us)

commit v2 on v1

--- a/solution.py
+++ b/solution.py
@@ -52,7 +52,7 @@
     )
 
 
-def call(body, outs, *args, scratch=(), smem=1, after=(), flops=0, bytes_accessed=0):
+def call(body, outs, *args, scratch=(), smem=1, after=(), flops=0, bytes_accessed=0, vmem=53):
     count = len(args)
     specs = [
         pl.BlockSpec(memory_space=pltpu.SMEM) if i < smem else pl.BlockSpec()
@@ -69,7 +69,7 @@
         in_specs=specs,
         out_specs=[pl.BlockSpec() for _ in outs],
         scratch_shapes=list(scratch),
-        compiler_params=pltpu.CompilerParams(vmem_limit_bytes=60 * 1024 * 1024),
+        compiler_params=pltpu.CompilerParams(vmem_limit_bytes=vmem * 1024 * 1024),
         cost_estimate=pl.CostEstimate(
             flops=flops, bytes_accessed=bytes_accessed, transcendentals=0
         ),
@@ -194,7 +194,7 @@
             ).astype(bf16)
             return carry
 
-        lax.fori_loop(0, HEADS // 4, pair_step, 0)
+        lax.fori_loop(0, HEADS // 4, pair_step, 0, unroll=True)
 
 
 def in_parts(value, rows):
@@ -508,17 +508,16 @@
     lax.fori_loop(0, HEADS // 4, pair_step, 0)
 
 
-def weights_backward(x_own, x_other, attn_in, grad_projected, weights, diagonals, keep, got, *refs):
-    whole, to_own, to_other = refs
-    whole[:, :QKV] = dot(attn_in[...], grad_projected[...], TN).astype(bf16)
+def weights_backward(attn_in, grad_projected, weights, diagonals, keep, got, whole):
+    sums = jnp.zeros((D, 1), f32)
+    for part in range(3):
+        columns = slice(part * HALF, (part + 1) * HALF)
+        grads = dot(attn_in[...], grad_projected[:, columns], TN)
+        whole[:, columns] = grads.astype(bf16)
+        sums = sums + jnp.sum(grads * weights[:, columns].astype(f32), axis=-1, keepdims=True)
+    extra_weights = weights[:, SENT - 128 :].astype(f32)
+    sums = sums / extra_weights[:, AT_ATTN : AT_ATTN + 1]
     whole[:, QKV : QKV + HALF] = (keep[:, :HALF].astype(f32) + got[...].astype(f32)).astype(bf16)
-    sums = jnp.zeros((D, 128), f32)
-    for block, (x_ref, out) in enumerate(((x_own, to_own), (x_other, to_other))):
-        rows = slice(block * TOK, (block + 1) * TOK)
-        grads = dot(grad_projected[rows], weights[:, :QKV], NT)
-        out[...] = grads
-        x = x_ref[...].astype(f32)
-        sums = sums + column_sums(grads * (x * inverse_rms(x)))
     buckets = diagonal_buckets()
     per_bucket = jnp.zeros((BUCKETS, 16), f32)
     for row in range(8):
@@ -529,6 +528,12 @@
     tall = lax.broadcasted_iota(jnp.int32, (D, 128), 1)
     extra = keep[:, HALF:].astype(f32) + dot(owner_rows(), per_bucket.astype(bf16), TN)
     whole[:, QKV + HALF :] = jnp.where(tall == AT_ATTN, sums, extra).astype(bf16)
+
+
+def input_grads(grad_projected, weights, to_own, to_other):
+    for block, out in enumerate((to_own, to_other)):
+        rows = slice(block * TOK, (block + 1) * TOK)
+        out[...] = dot(grad_projected[rows], weights[:, :QKV], NT)
 
 
 def input_backward(x_ref, grad_after, to_own, got, extras, grad_in):
@@ -597,6 +602,7 @@
         ffn_gain.reshape(1, 24),
         rel_bias,
         smem=0,
+        vmem=60,
     )
     weights1 = over_exp(packed).reshape(D, SENT)
     x_other = on_exp(hidden_in, SWAP)
@@ -712,11 +718,9 @@
         flops=9_000_000_000,
         bytes_accessed=8_000_000,
     )
-    whole, to_own, to_send = call(
+    (whole,) = call(
         weights_backward,
-        [((D, SENT), bf16), ((TOK, D), f32), ((TOK, D), f32)],
-        hidden_in,
-        x_other,
+        [((D, SENT), bf16)],
         attn_in,
         grad_projected,
         weights1,
@@ -724,10 +728,20 @@
         keep,
         got,
         smem=0,
-        flops=5_000_000_000,
+        flops=3_000_000_000,
         bytes_accessed=10_000_000,
     )
     parts = over_exp(hold_until(whole, returned).reshape(EXPERTS, 24, SENT))
+    to_own, to_send = call(
+        input_grads,
+        [((TOK, D), f32), ((TOK, D), f32)],
+        grad_projected,
+        weights1,
+        smem=0,
+        after=[returned, diagonals],
+        flops=1_000_000_000,
+        bytes_accessed=6_000_000,
+    )
     to_got = on_exp(to_send, SWAP)
     kept = run_expert_weights(
         group,

time: 237 us -> 226 us (0.954)
  Pallas kernels: 92 us -> 86.7 us
  local copies, waits for them, and re-layouts: 11.8 us -> 6.68 us
    pallas_call x11 -> x12, Pallas kernels: 53.4 us -> 48 us  [call(): pl.pallas_call(run, out_shape=[jax.ShapeDtypeStruct(shape, kind) for shap...]
    unnamed x43, local copies, waits for them, and re-layouts: 11.8 us -> 6.68 us
    all_to_all x5, starting transfers between devices: 30.2 us -> 27.7 us  [over_exp(): return lax.all_to_all(value, 'exp', split_axis=0, concat_axis=0, tiled=True)]
    all_to_all x5, waiting for transfers between devices: 52.9 us -> 55.3 us  [over_exp(): return lax.all_to_all(value, 'exp', split_axis=0, concat_axis=0, tiled=True)]
  transfers between devices with their start and end apart: 21 -> 21, of which waited for: 6 -> 7; matrix products, arithmetic and copies ran while one was open for 1% -> 0% of each run, Pallas kernels for 33% -> 33%
where the time goes in v2:
time: 226 us; the launch traced here: 225 us
  Pallas kernels  86.7 us (38%)
  waiting for transfers between devices  59.9 us (27%)
  starting transfers between devices  47.6 us (21%)
  blocking collectives  23.4 us (10%)
  local copies, waits for them, and re-layouts  6.68 us (3%)
    all_to_all x5, waiting for transfers between devices, over_exp(): return lax.all_to_all(value, 'exp', split_axis=0, concat_axis=0, tiled=True)  55.3 us
    pallas_call x12, Pallas kernels, call(): pl.pallas_call(run, out_shape=[jax.ShapeDtypeStruct(shape, kind) for shap...  48 us
    all_to_all x5, starting transfers between devices, over_exp(): return lax.all_to_all(value, 'exp', split_axis=0, concat_axis=0, tiled=True)  27.7 us
    all_to_all x1, blocking collectives, over_exp(): return lax.all_to_all(value, 'exp', split_axis=0, concat_axis=0, tiled=True)  23.4 us
    pallas_call x2, Pallas kernels, run_expert_weights(): pl.pallas_call(run, grid_spec=pltpu.PrefetchScalarGridSpec(num_scalar_pre...  22.1 us
    pallas_call x1, Pallas kernels, run_expert(): pl.pallas_call(run, grid=(FF // BLOCK,), in_specs=[wide, whole, pl.BlockS...  16.6 us
    ppermute x6, starting transfers between devices, over_groups(): return lax.ppermute(value, 'rep', z_shift(step))  12.1 us
    unnamed x43, local copies, waits for them, and re-layouts  6.68 us
  transfers between devices with their start and end apart: 21, of which 7 were waited for; matrix products, arithmetic and copies ran while one was open for 0% of the time, Pallas kernels for 33%

profile of v2, /device:TPU:0, one launch (start us, length us, event | category | flops | bytes accessed | tf_op | source)
XLA Modules:
  0.0 225.2 jit_solution(7996019692187509066)
XLA Ops:
  3.2 7.7 %all-to-all-start = ((bf16[32,24,1664]{2,1,0:T(8,128)(2,1)}), bf16[32,24,1664]{2,1,0:T(8,128)(2,1)}, u32[]{:S(2)}, u32[]{:S(2)}) async-start(bf16[32,24,1664]{2,1,0:T(8,128)(2,1)} %shard_map.229), calls=%async_computation | async-start | bytes 5111808 | tf_op jit(solution)/shard_map/all_to_all | solution.py:588
  14.3 31.8 %all-to-all-done = bf16[32,24,1664]{2,1,0:T(8,128)(2,1)} async-done(((bf16[32,24,1664]{2,1,0:T(8,128)(2,1)}), bf16[32,24,1664]{2,1,0:T(8,128)(2,1)}, u32[]{:S(2)}, u32[]{:S(2)}) %all-to-all-start) | async-done | bytes 2555936 | tf_op jit(solution)/shard_map/all_to_all | solution.py:588
  46.1 4.6 %all-to-all-start.1 = ((bf16[32,16,768]{2,1,0:T(8,128)(2,1)}), bf16[32,16,768]{2,1,0:T(8,128)(2,1)}, u32[]{:S(2)}, u32[]{:S(2)}) async-start(bf16[32,16,768]{2,1,0:T(8,128)(2,1)} %bitcast.30), calls=%async_computation.1 | async-start | bytes 1572864 | tf_op jit(solution)/shard_map/all_to_all | solution.py:588
  51.5 7.5 %shard_map.230 = (bf16[768,128]{1,0:T(8,128)(2,1)S(1)}, bf16[768,384]{1,0:T(8,128)(2,1)}, bf16[512,768]{1,0:T(8,128)(2,1)}, bf16[512,1152]{1,0:T(8,128)(2,1)}, b...) custom-call(s32[3]{0:T(128)S(1)} %pad_add_fusion.1.refs_0_, ...), custom_call_target="tpu_custom_call" | custom-call | flops 8999999488 | bytes 10000000 | tf_op jit(solution)/shard_map/pallas_call | solution.py:66
  62.0 3.3 %all-to-all-done.1 = bf16[32,16,768]{2,1,0:T(8,128)(2,1)} async-done(((bf16[32,16,768]{2,1,0:T(8,128)(2,1)}), bf16[32,16,768]{2,1,0:T(8,128)(2,1)}, u32[]{:S(2)}, u32[]{:S(2)}) %all-to-all-start.1) | async-done | bytes 786464 | tf_op jit(solution)/shard_map/all_to_all | solution.py:588
  65.3 4.3 %shard_map.233 = (bf16[768,768]{1,0:T(8,128)(2,1)}, f32[256,768]{1,0:T(8,128)}, bf16[256,768]{1,0:T(8,128)(2,1)}, f32[256,128]{1,0:T(8,128)S(1)}, f32[256,1]{1,0:T(8,128)S(1)}, /*index=5*/bf16[512,896]{1,0:T(8,128)(2,1)}) custom-call(s32[3]{0:T(128)S(1)} %pad_add_fusion.1.refs_0_, bf16[256,768]{1,0:T(8,128)(2,1)} %refs_0_.4, ...), custom_call_target="tpu_custom_call" | custom-call | flops 3000000000 | bytes 8000000 | tf_op jit(solution)/shard_map/pallas_call | solution.py:66
  69.7 4.8 %all-to-all-start.2 = ((bf16[32,16,896]{2,1,0:T(8,128)(2,1)}), bf16[32,16,896]{2,1,0:T(8,128)(2,1)S(1)}, u32[]{:S(2)}, u32[]{:S(2)}) async-start(bf16[32,16,896]{2,1,0:T(8,128)(2,1)} %bitcast.36), calls=%async_computation.2 | async-start | bytes 1835008 | tf_op jit(solution)/shard_map/all_to_all | solution.py:588
  78.7 11.7 %all-to-all-done.2 = bf16[32,16,896]{2,1,0:T(8,128)(2,1)S(1)} async-done(((bf16[32,16,896]{2,1,0:T(8,128)(2,1)}), bf16[32,16,896]{2,1,0:T(8,128)(2,1)S(1)}, u32[]{:S(2)}, u32[]{:S(2)}) %all-to-all-start.2) | async-done | bytes 917536 | tf_op jit(solution)/shard_map/all_to_all | solution.py:588
  94.5 2.8 %collective-permute-done.4.refs_4_ = bf16[512,768]{1,0:T(8,128)(2,1)} collective-permute-done((bf16[512,768]{1,0:T(8,128)(2,1)}, bf16[512,768]{1,0:T(8,128)(2,1)}, u32[]{:S(2)}, u32[]{:S(2)}) %collective-permute-start.4) | collective-permute-done | bytes 786464 | tf_op jit(solution)/shard_map/ppermute | solution.py:591
  97.2 16.6 %shard_map.234 = (bf16[512,768]{1,0:T(8,128)(2,1)}, bf16[512,896]{1,0:T(8,128)(2,1)}) custom-call(bf16[512,896]{1,0:T(8,128)(2,1)} %bitcast.33, bf16[512,768]{1,0:T(8,128)(2,1)} %bitcast.9.refs_9_.refs_1_.refs_3_, bf16[1,768,3072]{2,1,0:T(8,128)(2,1)} %refs_2_.8, bf16[1,3072,768]{2,1,0:T(8,128)(2,1)} %refs_3_.5, ...), custom_call_target="tpu_custom_call" | custom-call | flops 9663676416 | bytes 14680064 | tf_op jit(solution)/shard_map/pallas_call | solution.py:350
  113.9 23.4 %all_to_all.30 = bf16[32,16,896]{2,1,0:T(8,128)(2,1)} all-to-all(bf16[32,16,896]{2,1,0:T(8,128)(2,1)} %bitcast.38), channel_id=1, replica_groups=mesh['rep'=4,'exp'=32] {'exp'}, dimensions={0} | all-to-all | bytes 1835008 | tf_op jit(solution)/shard_map/all_to_all | solution.py:588
  138.3 5.9 %shard_map.235 = (f32[256,768]{1,0:T(8,128)}, bf16[256,384]{1,0:T(8,128)(2,1)S(1)}, bf16[256,384]{1,0:T(8,128)(2,1)S(1)}, bf16[768,512]{1,0:T(8,128)(2,1)}, bf16[768,384]{1,0:T(8,128)(2,1)}) custom-call(s32[3]{0:T(128)S(1)} %pad_add_fusion.1.refs_0_, s32[256,1]{1,0:T(8,128)S(1)} %copy.32.refs_0_.refs_2_.refs_1_, bf16[256,768]{1,0:T(8,128)(2,1)} %refs_2_.7, ...), custom_call_target="tpu_custom_call" | custom-call | flops 4000000000 | bytes 10000000 | tf_op jit(solution)/shard_map/pallas_call | solution.py:66
  144.3 3.9 %all-to-all-start.3 = ((bf16[32,16,768]{2,1,0:T(8,128)(2,1)}), bf16[32,16,768]{2,1,0:T(8,128)(2,1)S(1)}, u32[]{:S(2)}, u32[]{:S(2)}) async-start(bf16[32,16,768]{2,1,0:T(8,128)(2,1)} %bitcast.12), calls=%async_computation.3 | async-start | bytes 1572864 | tf_op jit(solution)/shard_map/all_to_all | solution.py:588
  148.5 7.0 %shard_map.236 = (bf16[512,1152]{1,0:T(8,128)(2,1)}, f32[16,8,512]{2,1,0:T(8,128)S(1)}) custom-call(s32[3]{0:T(128)S(1)} %pad_add_fusion.1.refs_0_, bf16[512,1152]{1,0:T(8,128)(2,1)} %get-tuple-element.60.refs_1_, bf16[12,256,256]{2,1,0:T(8,128)(2,1)} %get-tuple-element.61.refs_2_, bf16[256,384]{1,0:T(8,128)(2,1)S(1)} %get-tuple-element.66.refs_3_, ...), custom_call_target="tpu_custom_call" | custom-call | flops 8999999488 | bytes 8000000 | tf_op jit(solution)/shard_map/pallas_call | solution.py:66
  155.6 6.6 %shard_map.240.value = bf16[768,1664]{1,0:T(8,128)(2,1)} custom-call(bf16[512,768]{1,0:T(8,128)(2,1)} %get-tuple-element.73.refs_0_, bf16[512,1152]{1,0:T(8,128)(2,1)} %get-tuple-element.68.refs_0_.refs_1_, bf16[768,1664]{1,0:T(8,128)(2,1)} %bitcast.7.refs_5_.until.refs_1_.refs_2_, f32[16,8,512]{2,1,0:T(8,128)S(1)} %get-tuple-element.69.refs_3_, ...), custom_call_target="tpu_custom_call" | custom-call | flops 3000000000 | bytes 10000000 | tf_op jit(solution)/shard_map/pallas_call | solution.py:66
  163.7 6.7 %all-to-all-start.5 = ((bf16[32,24,1664]{2,1,0:T(8,128)(2,1)}), bf16[32,24,1664]{2,1,0:T(8,128)(2,1)S(1)}, u32[]{:S(2)}, u32[]{:S(2)}) async-start(bf16[32,24,1664]{2,1,0:T(8,128)(2,1)} %bitcast.29), calls=%async_computation.5 | async-start | bytes 5111808 | tf_op jit(solution)/shard_map/all_to_all | solution.py:588
  170.4 3.6 %collective-permute-start.14 = (bf16[512,896]{1,0:T(8,128)(2,1)}, bf16[512,896]{1,0:T(8,128)(2,1)}, u32[]{:S(2)}, u32[]{:S(2)}) collective-permute-start(bf16[512,896]{1,0:T(8,128)(2,1)} %bitcast.34), channel_id=1, source_target_pairs={{0,64},{32,96},{64,0},{96,32},{1,65},{33,97},{65,1},{97,33},{2,66}... | collective-permute-start | bytes 2752520 | tf_op jit(solution)/shard_map/ppermute | solution.py:591
  174.0 4.2 %shard_map.237 = (f32[256,768]{1,0:T(8,128)}, f32[256,768]{1,0:T(8,128)}) custom-call(bf16[512,1152]{1,0:T(8,128)(2,1)} %get-tuple-element.68.refs_0_.refs_1_, bf16[768,1664]{1,0:T(8,128)(2,1)} %bitcast.7.refs_5_.until.refs_1_.refs_2_, bf16[512,768]{1,0:T(8,128)(2,1)} %bitcast.27, f32[16,8,512]{2,1,0:T(8,128)S(1)} %get-tuple-element.69.refs_3_), custom_call_target="tpu_custom_call" | custom-call | flops 1000000000 | bytes 6000000 | tf_op jit(solution)/shard_map/pallas_call | solution.py:66
  178.5 2.5 %shard_map.238.refs_4_ = bf16[256,768]{1,0:T(8,128)(2,1)} custom-call(f32[256,768]{1,0:T(8,128)} %get-tuple-element.56.refs_5_.refs_0_, f32[256,1]{1,0:T(8,128)S(1)} %get-tuple-element.57.refs_8_.refs_1_, bf16[256,512]{1,0:T(8,128)(2,1)S(1)} %copy-done.6, bf16[512,768]{1,0:T(8,128)(2,1)} %bitcast.28, f32[256,768]{1,0:T(8,128)} %get-tuple-element.70.refs_4_.refs_8_), custom_call_target="tpu_custom_call" | custom-call | flops 200000000 | bytes 3000000 | tf_op jit(solution)/shard_map/pallas_call | solution.py:66
  181.0 14.0 %shard_map.242 = (f32[1,768,768]{2,1,0:T(8,128)}, f32[1,768,768]{2,1,0:T(8,128)}) custom-call(s32[1]{0:T(128)} %bitcast.17.pos, bf16[512,896]{1,0:T(8,128)(2,1)} %bitcast.35, bf16[512,896]{1,0:T(8,128)(2,1)} %copy-done.17, bf16[512,896]{1,0:T(8,128)(2,1)} %collective-permute-done.7.refs_14_.refs_2_, bf16[512,768]{1,0:T(8,128)(2,1)} %bitcast.9.refs_9_.refs_1_.refs_3_, ...), custom_call_target="tpu_custom_call" | custom-call | flops 7247757312 | bytes 14680064 | tf_op jit(solution)/shard_map/pallas_call | solution.py:385
  195.0 2.9 %shard_map.239.refs_3_ = f32[256,768]{1,0:T(8,128)} custom-call(bf16[256,768]{1,0:T(8,128)(2,1)S(1)} %copy-done.4, f32[256,768]{1,0:T(8,128)} %get-tuple-element.71.refs_1_, f32[256,768]{1,0:T(8,128)} %get-tuple-element.72.refs_2_, f32[256,768]{1,0:T(8,128)} %collective-permute-done.9.refs_3_, bf16[768,128]{1,0:T(8,128)(2,1)S(1)} %copy-done.8), custom_call_target="tpu_custom_call" | custom-call | flops 10000000 | bytes 5000000 | tf_op jit(solution)/shard_map/pallas_call | solution.py:66
  197.9 7.7 %all-to-all-done.5.refs_0_ = bf16[32,24,1664]{2,1,0:T(8,128)(2,1)S(1)} async-done(((bf16[32,24,1664]{2,1,0:T(8,128)(2,1)}), bf16[32,24,1664]{2,1,0:T(8,128)(2,1)S(1)}, u32[]{:S(2)}, u32[]{:S(2)}) %all-to-all-start.5) | async-done | bytes 2555936 | tf_op jit(solution)/shard_map/all_to_all | solution.py:588
  211.1 2.9 %collective-permute-start.12 = (bf16[24,3328]{1,0:T(8,128)(2,1)S(1)}, bf16[24,3328]{1,0:T(8,128)(2,1)S(1)}, u32[]{:S(2)}, u32[]{:S(2)}) collective-permute-start(bf16[24,3328]{1,0:T(8,128)(2,1)S(1)} %shard_map.243.refs_6_.refs_0_), channel_id=1, source_target_pairs={{0,64},{32,96},{64,0},{96,32},{1,65},{33,97},{65,1},{97,33},{2,66}... | collective-permute-start | bytes 479240 | tf_op jit(solution)/shard_map/ppermute | solution.py:791
  215.4 8.1 %shard_map.244 = (f32[1,768,768]{2,1,0:T(8,128)}, f32[1,768,768]{2,1,0:T(8,128)}) custom-call(s32[1]{0:T(128)} %bitcast.17.pos, bf16[512,896]{1,0:T(8,128)(2,1)} %collective-permute-done.14.refs_0_, bf16[512,768]{1,0:T(8,128)(2,1)} %collective-permute-done.15.refs_1_, bf16[1,768,3072]{2,1,0:T(8,128)(2,1)} %refs_2_.8, ...), custom_call_target="tpu_custom_call", output_to_operand_aliasing={{0}: (5, {}), {1}: (6, {})} | custom-call | flops 2415919104 | bytes 14680064 | tf_op jit(solution)/shard_map/pallas_call | solution.py:385
  (81 shorter events, 29.6 us)
Async XLA Ops:
  3.2 43.0 %all-to-all-start = ((bf16[32,24,1664]{2,1,0:T(8,128)(2,1)}), bf16[32,24,1664]{2,1,0:T(8,128)(2,1)}, u32[]{:S(2)}, u32[]{:S(2)}) async-start(bf16[32,24,1664]{2,1,0:T(8,128)(2,1)} %shard_map.229), calls=%async_computation | async-start | bytes 5111808 | tf_op jit(solution)/shard_map/all_to_all | solution.py:588
  10.8 39.9 %collective-permute-start = (bf16[256,768]{1,0:T(8,128)(2,1)S(1)}, bf16[256,768]{1,0:T(8,128)(2,1)S(1)}, u32[]{:S(2)}, u32[]{:S(2)}) collective-permute-start(bf16[256,768]{1,0:T(8,128)(2,1)S(1)} %copy-done.3), channel_id=1, source_target_pairs={{0,1},{1,0},{2,3},{3,2},{4,5},{5,4},{6,7},{7,6},{8,9},{9,8},{10,11... | collective-permute-start | bytes 1179656 | tf_op jit(solution)/shard_map/ppermute | solution.py:46
  11.1 3.0 %collective-permute-start.1 = (s32[256]{0:T(256)S(1)}, s32[256]{0:T(256)S(1)}, u32[]{:S(2)}, u32[]{:S(2)}) collective-permute-start(s32[256]{0:T(256)S(1)} %copy-done.16), channel_id=1, source_target_pairs={{0,1},{1,0},{2,3},{3,2},{4,5},{5,4},{6,7},{7,6},{8,9},{9,8},{10,11... | collective-permute-start | bytes 3080 | tf_op jit(solution)/shard_map/ppermute | solution.py:46
  46.1 19.2 %all-to-all-start.1 = ((bf16[32,16,768]{2,1,0:T(8,128)(2,1)}), bf16[32,16,768]{2,1,0:T(8,128)(2,1)}, u32[]{:S(2)}, u32[]{:S(2)}) async-start(bf16[32,16,768]{2,1,0:T(8,128)(2,1)} %bitcast.30), calls=%async_computation.1 | async-start | bytes 1572864 | tf_op jit(solution)/shard_map/all_to_all | solution.py:588
  59.7 2.3 %collective-permute-start.3 = (bf16[768,384]{1,0:T(8,128)(2,1)}, bf16[768,384]{1,0:T(8,128)(2,1)S(1)}, u32[]{:S(2)}, u32[]{:S(2)}) collective-permute-start(bf16[768,384]{1,0:T(8,128)(2,1)} %get-tuple-element.53.refs_6_), channel_id=1, source_target_pairs={{0,1},{1,0},{2,3},{3,2},{4,5},{5,4},{6,7},{7,6},{8,9},{9,8},{10,11... | collective-permute-start | bytes 1769480 | tf_op jit(solution)/shard_map/ppermute | solution.py:46
  59.8 2.2 collective-permute-start.2
  69.7 20.7 %all-to-all-start.2 = ((bf16[32,16,896]{2,1,0:T(8,128)(2,1)}), bf16[32,16,896]{2,1,0:T(8,128)(2,1)S(1)}, u32[]{:S(2)}, u32[]{:S(2)}) async-start(bf16[32,16,896]{2,1,0:T(8,128)(2,1)} %bitcast.36), calls=%async_computation.2 | async-start | bytes 1835008 | tf_op jit(solution)/shard_map/all_to_all | solution.py:588
  74.5 22.7 %collective-permute-start.4 = (bf16[512,768]{1,0:T(8,128)(2,1)}, bf16[512,768]{1,0:T(8,128)(2,1)}, u32[]{:S(2)}, u32[]{:S(2)}) collective-permute-start(bf16[512,768]{1,0:T(8,128)(2,1)} %bitcast.9.refs_9_.refs_1_.refs_3_), channel_id=1, source_target_pairs={{0,32},{32,64},{64,96},{96,0},{1,33},{33,65},{65,97},{97,1},{2,34}... | collective-permute-start | bytes 2359304 | tf_op jit(solution)/shard_map/ppermute | solution.py:591
  76.5 20.7 %collective-permute-start.5 = (bf16[512,768]{1,0:T(8,128)(2,1)}, bf16[512,768]{1,0:T(8,128)(2,1)}, u32[]{:S(2)}, u32[]{:S(2)}) collective-permute-start(bf16[512,768]{1,0:T(8,128)(2,1)} %bitcast.9.refs_9_.refs_1_.refs_3_), channel_id=1, source_target_pairs={{0,96},{32,0},{64,32},{96,64},{1,97},{33,1},{65,33},{97,65},{2,98}... | collective-permute-start | bytes 2359304 | tf_op jit(solution)/shard_map/ppermute | solution.py:591
  90.4 46.9 %collective-permute-start.6 = (bf16[512,896]{1,0:T(8,128)(2,1)S(1)}, bf16[512,896]{1,0:T(8,128)(2,1)S(1)}, u32[]{:S(2)}, u32[]{:S(2)}) collective-permute-start(bf16[512,896]{1,0:T(8,128)(2,1)S(1)} %bitcast.31), channel_id=1, source_target_pairs={{0,32},{32,64},{64,96},{96,0},{1,33},{33,65},{65,97},{97,1},{2,34}... | collective-permute-start | bytes 2752520 | tf_op jit(solution)/shard_map/ppermute | solution.py:591
  92.3 45.0 %collective-permute-start.7 = (bf16[512,896]{1,0:T(8,128)(2,1)S(1)}, bf16[512,896]{1,0:T(8,128)(2,1)}, u32[]{:S(2)}, u32[]{:S(2)}) collective-permute-start(bf16[512,896]{1,0:T(8,128)(2,1)S(1)} %bitcast.32), channel_id=1, source_target_pairs={{0,96},{32,0},{64,32},{96,64},{1,97},{33,1},{65,33},{97,65},{2,98}... | collective-permute-start | bytes 2752520 | tf_op jit(solution)/shard_map/ppermute | solution.py:591
  144.2 4.3 %collective-permute-start.8 = (bf16[256,384]{1,0:T(8,128)(2,1)S(1)}, bf16[256,384]{1,0:T(8,128)(2,1)S(1)}, u32[]{:S(2)}, u32[]{:S(2)}) collective-permute-start(bf16[256,384]{1,0:T(8,128)(2,1)S(1)} %get-tuple-element.67), channel_id=1, source_target_pairs={{0,1},{1,0},{2,3},{3,2},{4,5},{5,4},{6,7},{7,6},{8,9},{9,8},{10,11... | collective-permute-start | bytes 589832 | tf_op jit(solution)/shard_map/ppermute | solution.py:46
  144.3 18.5 %all-to-all-start.3 = ((bf16[32,16,768]{2,1,0:T(8,128)(2,1)}), bf16[32,16,768]{2,1,0:T(8,128)(2,1)S(1)}, u32[]{:S(2)}, u32[]{:S(2)}) async-start(bf16[32,16,768]{2,1,0:T(8,128)(2,1)} %bitcast.12), calls=%async_computation.3 | async-start | bytes 1572864 | tf_op jit(solution)/shard_map/all_to_all | solution.py:588
  148.2 7.3 %collective-permute-start.10 = (bf16[768,384]{1,0:T(8,128)(2,1)}, bf16[768,384]{1,0:T(8,128)(2,1)S(1)}, u32[]{:S(2)}, u32[]{:S(2)}) collective-permute-start(bf16[768,384]{1,0:T(8,128)(2,1)} %get-tuple-element.75), channel_id=1, source_target_pairs={{0,1},{1,0},{2,3},{3,2},{4,5},{5,4},{6,7},{7,6},{8,9},{9,8},{10,11... | collective-permute-start | bytes 1769480 | tf_op jit(solution)/shard_map/ppermute | solution.py:46
  163.7 42.0 %all-to-all-start.5 = ((bf16[32,24,1664]{2,1,0:T(8,128)(2,1)}), bf16[32,24,1664]{2,1,0:T(8,128)(2,1)S(1)}, u32[]{:S(2)}, u32[]{:S(2)}) async-start(bf16[32,24,1664]{2,1,0:T(8,128)(2,1)} %bitcast.29), calls=%async_computation.5 | async-start | bytes 5111808 | tf_op jit(solution)/shard_map/all_to_all | solution.py:588
  170.4 45.1 %collective-permute-start.14 = (bf16[512,896]{1,0:T(8,128)(2,1)}, bf16[512,896]{1,0:T(8,128)(2,1)}, u32[]{:S(2)}, u32[]{:S(2)}) collective-permute-start(bf16[512,896]{1,0:T(8,128)(2,1)} %bitcast.34), channel_id=1, source_target_pairs={{0,64},{32,96},{64,0},{96,32},{1,65},{33,97},{65,1},{97,33},{2,66}... | collective-permute-start | bytes 2752520 | tf_op jit(solution)/shard_map/ppermute | solution.py:591
  178.2 16.8 %collective-permute-start.9 = (f32[256,768]{1,0:T(8,128)}, f32[256,768]{1,0:T(8,128)}, u32[]{:S(2)}, u32[]{:S(2)}) collective-permute-start(f32[256,768]{1,0:T(8,128)} %get-tuple-element.70.refs_4_.refs_8_), channel_id=1, source_target_pairs={{0,1},{1,0},{2,3},{3,2},{4,5},{5,4},{6,7},{7,6},{8,9},{9,8},{10,11... | collective-permute-start | bytes 2359304 | tf_op jit(solution)/shard_map/ppermute | solution.py:46
  178.2 37.2 %collective-permute-start.15 = (bf16[512,768]{1,0:T(8,128)(2,1)}, bf16[512,768]{1,0:T(8,128)(2,1)}, u32[]{:S(2)}, u32[]{:S(2)}) collective-permute-start(bf16[512,768]{1,0:T(8,128)(2,1)} %bitcast.9.refs_9_.refs_1_.refs_3_), channel_id=1, source_target_pairs={{0,64},{32,96},{64,0},{96,32},{1,65},{33,97},{65,1},{97,33},{2,66}... | collective-permute-start | bytes 2359304 | tf_op jit(solution)/shard_map/ppermute | solution.py:591
  181.0 14.0 %copy-start.4 = (bf16[256,768]{1,0:T(8,128)(2,1)S(1)}, bf16[256,768]{1,0:T(8,128)(2,1)}, u32[]{:S(2)}) copy-start(bf16[256,768]{1,0:T(8,128)(2,1)} %refs_0_.4) | copy-start | bytes 1179652
  181.0 14.0 %copy-start.8 = (bf16[768,128]{1,0:T(8,128)(2,1)S(1)}, bf16[768,128]{1,0:T(8,128)(2,1)}, u32[]{:S(2)}) copy-start(bf16[768,128]{1,0:T(8,128)(2,1)} %copy-done.7) | copy-start | bytes 589828
  195.0 12.2 %copy-start = (bf16[256,768]{1,0:T(8,128)(2,1)S(1)}, bf16[256,768]{1,0:T(8,128)(2,1)}, u32[]{:S(2)}) copy-start(bf16[256,768]{1,0:T(8,128)(2,1)} %shard_map.238.refs_4_) | copy-start | bytes 1179652
  209.2 14.4 %collective-permute-start.11 = (bf16[24,3328]{1,0:T(8,128)(2,1)S(1)}, bf16[24,3328]{1,0:T(8,128)(2,1)S(1)}, u32[]{:S(2)}, u32[]{:S(2)}) collective-permute-start(bf16[24,3328]{1,0:T(8,128)(2,1)S(1)} %shard_map.243.refs_6_.refs_0_), channel_id=1, source_target_pairs={{0,32},{32,64},{64,96},{96,0},{1,33},{33,65},{65,97},{97,1},{2,34}... | collective-permute-start | bytes 479240 | tf_op jit(solution)/shard_map/ppermute | solution.py:791
  211.1 12.4 %collective-permute-start.12 = (bf16[24,3328]{1,0:T(8,128)(2,1)S(1)}, bf16[24,3328]{1,0:T(8,128)(2,1)S(1)}, u32[]{:S(2)}, u32[]{:S(2)}) collective-permute-start(bf16[24,3328]{1,0:T(8,128)(2,1)S(1)} %shard_map.243.refs_6_.refs_0_), channel_id=1, source_target_pairs={{0,64},{32,96},{64,0},{96,32},{1,65},{33,97},{65,1},{97,33},{2,66}... | collective-permute-start | bytes 479240 | tf_op jit(solution)/shard_map/ppermute | solution.py:791
  214.1 9.5 %collective-permute-start.13 = (bf16[24,3328]{1,0:T(8,128)(2,1)S(1)}, bf16[24,3328]{1,0:T(8,128)(2,1)S(1)}, u32[]{:S(2)}, u32[]{:S(2)}) collective-permute-start(bf16[24,3328]{1,0:T(8,128)(2,1)S(1)} %shard_map.243.refs_6_.refs_0_), channel_id=1, source_target_pairs={{0,96},{32,0},{64,32},{96,64},{1,97},{33,1},{65,33},{97,65},{2,98}... | collective-permute-start | bytes 479240 | tf_op jit(solution)/shard_map/ppermute | solution.py:791
  (17 other events, 81.1 us)

commit v3 on v2

--- a/solution.py
+++ b/solution.py
@@ -52,7 +52,7 @@
     )
 
 
-def call(body, outs, *args, scratch=(), smem=1, after=(), flops=0, bytes_accessed=0, vmem=53):
+def call(body, outs, *args, scratch=(), smem=1, after=(), flops=0, bytes_accessed=0, vmem=52):
     count = len(args)
     specs = [
         pl.BlockSpec(memory_space=pltpu.SMEM) if i < smem else pl.BlockSpec()

time: 226 us -> 224 us (level)
  Pallas kernels: 86.7 us -> 81.7 us
  waiting for transfers between devices: 59.9 us -> 63.5 us
    pallas_call x12, Pallas kernels: 48 us -> 42.9 us  [call(): pl.pallas_call(run, out_shape=[jax.ShapeDtypeStruct(shape, kind) for shap...]
    all_to_all x5, waiting for transfers between devices: 55.3 us -> 58.9 us  [over_exp(): return lax.all_to_all(value, 'exp', split_axis=0, concat_axis=0, tiled=True)]
    unnamed x43 -> x45, local copies, waits for them, and re-layouts: 6.68 us -> 6.61 us
  transfers between devices with their start and end apart: 21 -> 21, of which waited for: 7 -> 7; matrix products, arithmetic and copies ran while one was open for 0% -> 0% of each run, Pallas kernels for 33% -> 31%
where the time goes in v3:
time: 224 us; the launch traced here: 223 us
  Pallas kernels  81.7 us (36%)
  waiting for transfers between devices  63.5 us (28%)
  starting transfers between devices  46.6 us (21%)
  blocking collectives  23.4 us (10%)
  local copies, waits for them, and re-layouts  6.61 us (3%)
    all_to_all x5, waiting for transfers between devices, over_exp(): return lax.all_to_all(value, 'exp', split_axis=0, concat_axis=0, tiled=True)  58.9 us
    pallas_call x12, Pallas kernels, call(): pl.pallas_call(run, out_shape=[jax.ShapeDtypeStruct(shape, kind) for shap...  42.9 us
    all_to_all x5, starting transfers between devices, over_exp(): return lax.all_to_all(value, 'exp', split_axis=0, concat_axis=0, tiled=True)  26.7 us
    all_to_all x1, blocking collectives, over_exp(): return lax.all_to_all(value, 'exp', split_axis=0, concat_axis=0, tiled=True)  23.4 us
    pallas_call x2, Pallas kernels, run_expert_weights(): pl.pallas_call(run, grid_spec=pltpu.PrefetchScalarGridSpec(num_scalar_pre...  22.1 us
    pallas_call x1, Pallas kernels, run_expert(): pl.pallas_call(run, grid=(FF // BLOCK,), in_specs=[wide, whole, pl.BlockS...  16.7 us
    ppermute x6, starting transfers between devices, over_groups(): return lax.ppermute(value, 'rep', z_shift(step))  12.2 us
    unnamed x45, local copies, waits for them, and re-layouts  6.61 us
  transfers between devices with their start and end apart: 21, of which 7 were waited for; matrix products, arithmetic and copies ran while one was open for 0% of the time, Pallas kernels for 31%

profile of v3, /device:TPU:0, one launch (start us, length us, event | category | flops | bytes accessed | tf_op | source)
XLA Modules:
  0.0 222.8 jit_solution(2092966723609016238)
XLA Ops:
  0.6 2.5 %shard_map.229 = bf16[32,24,1664]{2,1,0:T(8,128)(2,1)} custom-call(bf16[24,768]{1,0:T(8,128)(2,1)} %refs_0_.3, bf16[24,768]{1,0:T(8,128)(2,1)} %refs_1_.5, bf16[24,768]{1,0:T(8,128)(2,1)} %refs_2_.5, bf16[24,768]{1,0:T(8,128)(2,1)} %refs_3_.3, bf16[24,32]{1,0:T(8,128)(2,1)} %refs_4_.1, bf16[1,24]{1,0:T(2,128)(2,1)} %bitcast.42, bf16[1,24]{1,0:T(2,128)(2,1)} %bitcast.43, ...), custom_call_target="tpu_custom_call" | custom-call | tf_op jit(solution)/shard_map/pallas_call | solution.py:66
  3.2 7.7 %all-to-all-start = ((bf16[32,24,1664]{2,1,0:T(8,128)(2,1)}), bf16[32,24,1664]{2,1,0:T(8,128)(2,1)}, u32[]{:S(2)}, u32[]{:S(2)}) async-start(bf16[32,24,1664]{2,1,0:T(8,128)(2,1)} %shard_map.229), calls=%async_computation | async-start | bytes 5111808 | tf_op jit(solution)/shard_map/all_to_all | solution.py:588
  13.6 32.5 %all-to-all-done = bf16[32,24,1664]{2,1,0:T(8,128)(2,1)} async-done(((bf16[32,24,1664]{2,1,0:T(8,128)(2,1)}), bf16[32,24,1664]{2,1,0:T(8,128)(2,1)}, u32[]{:S(2)}, u32[]{:S(2)}) %all-to-all-start) | async-done | bytes 2555936 | tf_op jit(solution)/shard_map/all_to_all | solution.py:588
  46.2 4.6 %all-to-all-start.1 = ((bf16[32,16,768]{2,1,0:T(8,128)(2,1)}), bf16[32,16,768]{2,1,0:T(8,128)(2,1)}, u32[]{:S(2)}, u32[]{:S(2)}) async-start(bf16[32,16,768]{2,1,0:T(8,128)(2,1)} %bitcast.28), calls=%async_computation.1 | async-start | bytes 1572864 | tf_op jit(solution)/shard_map/all_to_all | solution.py:588
  50.8 7.2 %shard_map.230 = (bf16[768,128]{1,0:T(8,128)(2,1)S(1)}, bf16[768,384]{1,0:T(8,128)(2,1)}, bf16[512,768]{1,0:T(8,128)(2,1)}, bf16[512,1152]{1,0:T(8,128)(2,1)}, b...) custom-call(s32[3]{0:T(128)S(1)} %pad_add_fusion.1.refs_0_, ...), custom_call_target="tpu_custom_call" | custom-call | flops 8999999488 | bytes 10000000 | tf_op jit(solution)/shard_map/pallas_call | solution.py:66
  60.3 5.0 %all-to-all-done.1 = bf16[32,16,768]{2,1,0:T(8,128)(2,1)} async-done(((bf16[32,16,768]{2,1,0:T(8,128)(2,1)}), bf16[32,16,768]{2,1,0:T(8,128)(2,1)}, u32[]{:S(2)}, u32[]{:S(2)}) %all-to-all-start.1) | async-done | bytes 786464 | tf_op jit(solution)/shard_map/all_to_all | solution.py:588
  65.4 4.4 %shard_map.233 = (bf16[768,768]{1,0:T(8,128)(2,1)}, f32[256,768]{1,0:T(8,128)}, bf16[256,768]{1,0:T(8,128)(2,1)S(1)}, f32[256,128]{1,0:T(8,128)S(1)}, f32[256,1]{1,0:T(8,128)S(1)}, /*index=5*/bf16[512,896]{1,0:T(8,128)(2,1)}) custom-call(s32[3]{0:T(128)S(1)} %pad_add_fusion.1.refs_0_, bf16[256,768]{1,0:T(8,128)(2,1)} %refs_0_.4, ...), custom_call_target="tpu_custom_call" | custom-call | flops 3000000000 | bytes 8000000 | tf_op jit(solution)/shard_map/pallas_call | solution.py:66
  69.8 3.9 %all-to-all-start.2 = ((bf16[32,16,896]{2,1,0:T(8,128)(2,1)}), bf16[32,16,896]{2,1,0:T(8,128)(2,1)S(1)}, u32[]{:S(2)}, u32[]{:S(2)}) async-start(bf16[32,16,896]{2,1,0:T(8,128)(2,1)} %bitcast.36), calls=%async_computation.2 | async-start | bytes 1835008 | tf_op jit(solution)/shard_map/all_to_all | solution.py:588
  77.9 11.7 %all-to-all-done.2 = bf16[32,16,896]{2,1,0:T(8,128)(2,1)S(1)} async-done(((bf16[32,16,896]{2,1,0:T(8,128)(2,1)}), bf16[32,16,896]{2,1,0:T(8,128)(2,1)S(1)}, u32[]{:S(2)}, u32[]{:S(2)}) %all-to-all-start.2) | async-done | bytes 917536 | tf_op jit(solution)/shard_map/all_to_all | solution.py:588
  93.7 2.8 %collective-permute-done.4.refs_4_ = bf16[512,768]{1,0:T(8,128)(2,1)} collective-permute-done((bf16[512,768]{1,0:T(8,128)(2,1)}, bf16[512,768]{1,0:T(8,128)(2,1)}, u32[]{:S(2)}, u32[]{:S(2)}) %collective-permute-start.4) | collective-permute-done | bytes 786464 | tf_op jit(solution)/shard_map/ppermute | solution.py:591
  96.5 16.7 %shard_map.234 = (bf16[512,768]{1,0:T(8,128)(2,1)}, bf16[512,896]{1,0:T(8,128)(2,1)}) custom-call(bf16[512,896]{1,0:T(8,128)(2,1)} %bitcast.33, bf16[512,768]{1,0:T(8,128)(2,1)} %bitcast.9.refs_9_.refs_1_.refs_3_, bf16[1,768,3072]{2,1,0:T(8,128)(2,1)} %refs_2_.8, bf16[1,3072,768]{2,1,0:T(8,128)(2,1)} %refs_3_.5, ...), custom_call_target="tpu_custom_call" | custom-call | flops 9663676416 | bytes 14680064 | tf_op jit(solution)/shard_map/pallas_call | solution.py:350
  113.1 23.4 %all_to_all.30 = bf16[32,16,896]{2,1,0:T(8,128)(2,1)} all-to-all(bf16[32,16,896]{2,1,0:T(8,128)(2,1)} %bitcast.38), channel_id=1, replica_groups=mesh['rep'=4,'exp'=32] {'exp'}, dimensions={0} | all-to-all | bytes 1835008 | tf_op jit(solution)/shard_map/all_to_all | solution.py:588
  136.6 5.7 %shard_map.235 = (f32[256,768]{1,0:T(8,128)}, bf16[256,384]{1,0:T(8,128)(2,1)S(1)}, bf16[256,384]{1,0:T(8,128)(2,1)S(1)}, bf16[768,512]{1,0:T(8,128)(2,1)}, bf16[768,384]{1,0:T(8,128)(2,1)}) custom-call(s32[3]{0:T(128)S(1)} %pad_add_fusion.1.refs_0_, s32[256,1]{1,0:T(8,128)S(1)} %copy.32.refs_0_.refs_2_.refs_1_, bf16[256,768]{1,0:T(8,128)(2,1)} %refs_2_.7, ...), custom_call_target="tpu_custom_call" | custom-call | flops 4000000000 | bytes 10000000 | tf_op jit(solution)/shard_map/pallas_call | solution.py:66
  142.3 3.9 %all-to-all-start.3 = ((bf16[32,16,768]{2,1,0:T(8,128)(2,1)}), bf16[32,16,768]{2,1,0:T(8,128)(2,1)S(1)}, u32[]{:S(2)}, u32[]{:S(2)}) async-start(bf16[32,16,768]{2,1,0:T(8,128)(2,1)} %bitcast.12), calls=%async_computation.3 | async-start | bytes 1572864 | tf_op jit(solution)/shard_map/all_to_all | solution.py:588
  146.5 6.1 %shard_map.236 = (bf16[512,1152]{1,0:T(8,128)(2,1)S(1)}, f32[16,8,512]{2,1,0:T(8,128)S(1)}) custom-call(s32[3]{0:T(128)S(1)} %pad_add_fusion.1.refs_0_, bf16[512,1152]{1,0:T(8,128)(2,1)} %get-tuple-element.60.refs_1_, bf16[12,256,256]{2,1,0:T(8,128)(2,1)} %get-tuple-element.61.refs_2_, bf16[256,384]{1,0:T(8,128)(2,1)S(1)} %get-tuple-element.66.refs_3_, ...), custom_call_target="tpu_custom_call" | custom-call | flops 8999999488 | bytes 8000000 | tf_op jit(solution)/shard_map/pallas_call | solution.py:66
  153.7 6.2 %shard_map.240.value = bf16[768,1664]{1,0:T(8,128)(2,1)} custom-call(bf16[512,768]{1,0:T(8,128)(2,1)S(1)} %copy-done.15, bf16[512,1152]{1,0:T(8,128)(2,1)} %copy-done.7, bf16[768,1664]{1,0:T(8,128)(2,1)} %bitcast.7.refs_5_.until.refs_1_.refs_2_, f32[16,8,512]{2,1,0:T(8,128)S(1)} %get-tuple-element.69.refs_3_, bf16[768,512]{1,0:T(8,128)(2,1)} %get-tuple-element.74.refs_4_, ...), custom_call_target="tpu_custom_call" | custom-call | flops 3000000000 | bytes 10000000 | tf_op jit(solution)/shard_map/pallas_call | solution.py:66
  161.7 6.6 %all-to-all-start.5 = ((bf16[32,24,1664]{2,1,0:T(8,128)(2,1)}), bf16[32,24,1664]{2,1,0:T(8,128)(2,1)}, u32[]{:S(2)}, u32[]{:S(2)}) async-start(bf16[32,24,1664]{2,1,0:T(8,128)(2,1)} %bitcast.30), calls=%async_computation.5 | async-start | bytes 5111808 | tf_op jit(solution)/shard_map/all_to_all | solution.py:588
  168.3 3.6 %collective-permute-start.14 = (bf16[512,896]{1,0:T(8,128)(2,1)}, bf16[512,896]{1,0:T(8,128)(2,1)}, u32[]{:S(2)}, u32[]{:S(2)}) collective-permute-start(bf16[512,896]{1,0:T(8,128)(2,1)} %bitcast.34), channel_id=1, source_target_pairs={{0,64},{32,96},{64,0},{96,32},{1,65},{33,97},{65,1},{97,33},{2,66}... | collective-permute-start | bytes 2752520 | tf_op jit(solution)/shard_map/ppermute | solution.py:591
  171.9 3.3 %shard_map.237 = (f32[256,768]{1,0:T(8,128)S(1)}, f32[256,768]{1,0:T(8,128)S(1)}) custom-call(bf16[512,1152]{1,0:T(8,128)(2,1)} %copy-done.7, bf16[768,1664]{1,0:T(8,128)(2,1)} %bitcast.7.refs_5_.until.refs_1_.refs_2_, bf16[512,768]{1,0:T(8,128)(2,1)} %bitcast.26, f32[16,8,512]{2,1,0:T(8,128)S(1)} %get-tuple-element.69.refs_3_), custom_call_target="tpu_custom_call" | custom-call | flops 1000000000 | bytes 6000000 | tf_op jit(solution)/shard_map/pallas_call | solution.py:66
  178.1 14.0 %shard_map.242 = (f32[1,768,768]{2,1,0:T(8,128)}, f32[1,768,768]{2,1,0:T(8,128)}) custom-call(s32[1]{0:T(128)} %bitcast.17.pos, bf16[512,896]{1,0:T(8,128)(2,1)} %bitcast.35, bf16[512,896]{1,0:T(8,128)(2,1)} %collective-permute-done.6.refs_13_.refs_1_, bf16[512,896]{1,0:T(8,128)(2,1)} %collective-permute-done.7.refs_14_.refs_2_, ...), custom_call_target="tpu_custom_call" | custom-call | flops 7247757312 | bytes 14680064 | tf_op jit(solution)/shard_map/pallas_call | solution.py:385
  192.2 2.7 %shard_map.239.refs_3_ = f32[256,768]{1,0:T(8,128)} custom-call(bf16[256,768]{1,0:T(8,128)(2,1)S(1)} %copy-done.13, f32[256,768]{1,0:T(8,128)S(1)} %copy-done.8, f32[256,768]{1,0:T(8,128)} %copy-done.9, f32[256,768]{1,0:T(8,128)} %collective-permute-done.9.refs_3_, bf16[768,128]{1,0:T(8,128)(2,1)S(1)} %get-tuple-element.54.refs_8_.refs_12_.refs_4_), custom_call_target="tpu_custom_call" | custom-call | flops 10000000 | bytes 5000000 | tf_op jit(solution)/shard_map/pallas_call | solution.py:66
  194.9 8.7 %all-to-all-done.5.refs_0_ = bf16[32,24,1664]{2,1,0:T(8,128)(2,1)} async-done(((bf16[32,24,1664]{2,1,0:T(8,128)(2,1)}), bf16[32,24,1664]{2,1,0:T(8,128)(2,1)}, u32[]{:S(2)}, u32[]{:S(2)}) %all-to-all-start.5) | async-done | bytes 2555936 | tf_op jit(solution)/shard_map/all_to_all | solution.py:588
  208.7 2.9 %collective-permute-start.12 = (bf16[24,3328]{1,0:T(8,128)(2,1)S(1)}, bf16[24,3328]{1,0:T(8,128)(2,1)S(1)}, u32[]{:S(2)}, u32[]{:S(2)}) collective-permute-start(bf16[24,3328]{1,0:T(8,128)(2,1)S(1)} %shard_map.243.refs_6_.refs_0_), channel_id=1, source_target_pairs={{0,64},{32,96},{64,0},{96,32},{1,65},{33,97},{65,1},{97,33},{2,66}... | collective-permute-start | bytes 479240 | tf_op jit(solution)/shard_map/ppermute | solution.py:791
  213.0 8.1 %shard_map.244 = (f32[1,768,768]{2,1,0:T(8,128)}, f32[1,768,768]{2,1,0:T(8,128)}) custom-call(s32[1]{0:T(128)} %bitcast.17.pos, bf16[512,896]{1,0:T(8,128)(2,1)} %collective-permute-done.14.refs_0_, bf16[512,768]{1,0:T(8,128)(2,1)} %collective-permute-done.15.refs_1_, bf16[1,768,3072]{2,1,0:T(8,128)(2,1)} %refs_2_.8, ...), custom_call_target="tpu_custom_call", output_to_operand_aliasing={{0}: (5, {}), {1}: (6, {})} | custom-call | flops 2415919104 | bytes 14680064 | tf_op jit(solution)/shard_map/pallas_call | solution.py:385
  (83 shorter events, 27.5 us)
Async XLA Ops:
  3.2 43.0 %all-to-all-start = ((bf16[32,24,1664]{2,1,0:T(8,128)(2,1)}), bf16[32,24,1664]{2,1,0:T(8,128)(2,1)}, u32[]{:S(2)}, u32[]{:S(2)}) async-start(bf16[32,24,1664]{2,1,0:T(8,128)(2,1)} %shard_map.229), calls=%async_computation | async-start | bytes 5111808 | tf_op jit(solution)/shard_map/all_to_all | solution.py:588
  10.9 39.9 %collective-permute-start = (bf16[256,768]{1,0:T(8,128)(2,1)S(1)}, bf16[256,768]{1,0:T(8,128)(2,1)S(1)}, u32[]{:S(2)}, u32[]{:S(2)}) collective-permute-start(bf16[256,768]{1,0:T(8,128)(2,1)S(1)} %copy-done.12), channel_id=1, source_target_pairs={{0,1},{1,0},{2,3},{3,2},{4,5},{5,4},{6,7},{7,6},{8,9},{9,8},{10,11... | collective-permute-start | bytes 1179656 | tf_op jit(solution)/shard_map/ppermute | solution.py:46
  11.2 2.3 %collective-permute-start.1 = (s32[256]{0:T(256)S(1)}, s32[256]{0:T(256)S(1)}, u32[]{:S(2)}, u32[]{:S(2)}) collective-permute-start(s32[256]{0:T(256)S(1)} %copy-done.19), channel_id=1, source_target_pairs={{0,1},{1,0},{2,3},{3,2},{4,5},{5,4},{6,7},{7,6},{8,9},{9,8},{10,11... | collective-permute-start | bytes 3080 | tf_op jit(solution)/shard_map/ppermute | solution.py:46
  46.2 19.2 %all-to-all-start.1 = ((bf16[32,16,768]{2,1,0:T(8,128)(2,1)}), bf16[32,16,768]{2,1,0:T(8,128)(2,1)}, u32[]{:S(2)}, u32[]{:S(2)}) async-start(bf16[32,16,768]{2,1,0:T(8,128)(2,1)} %bitcast.28), calls=%async_computation.1 | async-start | bytes 1572864 | tf_op jit(solution)/shard_map/all_to_all | solution.py:588
  58.0 2.3 %collective-permute-start.3 = (bf16[768,384]{1,0:T(8,128)(2,1)}, bf16[768,384]{1,0:T(8,128)(2,1)S(1)}, u32[]{:S(2)}, u32[]{:S(2)}) collective-permute-start(bf16[768,384]{1,0:T(8,128)(2,1)} %get-tuple-element.53.refs_6_), channel_id=1, source_target_pairs={{0,1},{1,0},{2,3},{3,2},{4,5},{5,4},{6,7},{7,6},{8,9},{9,8},{10,11... | collective-permute-start | bytes 1769480 | tf_op jit(solution)/shard_map/ppermute | solution.py:46
  58.1 2.2 collective-permute-start.2
  69.8 43.3 %copy-start.16 = (bf16[256,768]{1,0:T(8,128)(2,1)}, bf16[256,768]{1,0:T(8,128)(2,1)S(1)}, u32[]{:S(2)}) copy-start(bf16[256,768]{1,0:T(8,128)(2,1)S(1)} %get-tuple-element.62.refs_6_) | copy-start | bytes 1179652
  69.8 19.9 %all-to-all-start.2 = ((bf16[32,16,896]{2,1,0:T(8,128)(2,1)}), bf16[32,16,896]{2,1,0:T(8,128)(2,1)S(1)}, u32[]{:S(2)}, u32[]{:S(2)}) async-start(bf16[32,16,896]{2,1,0:T(8,128)(2,1)} %bitcast.36), calls=%async_computation.2 | async-start | bytes 1835008 | tf_op jit(solution)/shard_map/all_to_all | solution.py:588
  73.7 22.8 %collective-permute-start.4 = (bf16[512,768]{1,0:T(8,128)(2,1)}, bf16[512,768]{1,0:T(8,128)(2,1)}, u32[]{:S(2)}, u32[]{:S(2)}) collective-permute-start(bf16[512,768]{1,0:T(8,128)(2,1)} %bitcast.9.refs_9_.refs_1_.refs_3_), channel_id=1, source_target_pairs={{0,32},{32,64},{64,96},{96,0},{1,33},{33,65},{65,97},{97,1},{2,34}... | collective-permute-start | bytes 2359304 | tf_op jit(solution)/shard_map/ppermute | solution.py:591
  75.7 20.8 %collective-permute-start.5 = (bf16[512,768]{1,0:T(8,128)(2,1)}, bf16[512,768]{1,0:T(8,128)(2,1)}, u32[]{:S(2)}, u32[]{:S(2)}) collective-permute-start(bf16[512,768]{1,0:T(8,128)(2,1)} %bitcast.9.refs_9_.refs_1_.refs_3_), channel_id=1, source_target_pairs={{0,96},{32,0},{64,32},{96,64},{1,97},{33,1},{65,33},{97,65},{2,98}... | collective-permute-start | bytes 2359304 | tf_op jit(solution)/shard_map/ppermute | solution.py:591
  89.7 46.9 %collective-permute-start.6 = (bf16[512,896]{1,0:T(8,128)(2,1)S(1)}, bf16[512,896]{1,0:T(8,128)(2,1)}, u32[]{:S(2)}, u32[]{:S(2)}) collective-permute-start(bf16[512,896]{1,0:T(8,128)(2,1)S(1)} %bitcast.31), channel_id=1, source_target_pairs={{0,32},{32,64},{64,96},{96,0},{1,33},{33,65},{65,97},{97,1},{2,34}... | collective-permute-start | bytes 2752520 | tf_op jit(solution)/shard_map/ppermute | solution.py:591
  91.6 45.0 %collective-permute-start.7 = (bf16[512,896]{1,0:T(8,128)(2,1)S(1)}, bf16[512,896]{1,0:T(8,128)(2,1)}, u32[]{:S(2)}, u32[]{:S(2)}) collective-permute-start(bf16[512,896]{1,0:T(8,128)(2,1)S(1)} %bitcast.32), channel_id=1, source_target_pairs={{0,96},{32,0},{64,32},{96,64},{1,97},{33,1},{65,33},{97,65},{2,98}... | collective-permute-start | bytes 2752520 | tf_op jit(solution)/shard_map/ppermute | solution.py:591
  142.2 4.3 %collective-permute-start.8 = (bf16[256,384]{1,0:T(8,128)(2,1)S(1)}, bf16[256,384]{1,0:T(8,128)(2,1)S(1)}, u32[]{:S(2)}, u32[]{:S(2)}) collective-permute-start(bf16[256,384]{1,0:T(8,128)(2,1)S(1)} %get-tuple-element.67), channel_id=1, source_target_pairs={{0,1},{1,0},{2,3},{3,2},{4,5},{5,4},{6,7},{7,6},{8,9},{9,8},{10,11... | collective-permute-start | bytes 589832 | tf_op jit(solution)/shard_map/ppermute | solution.py:46
  142.3 18.5 %all-to-all-start.3 = ((bf16[32,16,768]{2,1,0:T(8,128)(2,1)}), bf16[32,16,768]{2,1,0:T(8,128)(2,1)S(1)}, u32[]{:S(2)}, u32[]{:S(2)}) async-start(bf16[32,16,768]{2,1,0:T(8,128)(2,1)} %bitcast.12), calls=%async_computation.3 | async-start | bytes 1572864 | tf_op jit(solution)/shard_map/all_to_all | solution.py:588
  146.2 7.4 %collective-permute-start.10 = (bf16[768,384]{1,0:T(8,128)(2,1)}, bf16[768,384]{1,0:T(8,128)(2,1)S(1)}, u32[]{:S(2)}, u32[]{:S(2)}) collective-permute-start(bf16[768,384]{1,0:T(8,128)(2,1)} %get-tuple-element.75), channel_id=1, source_target_pairs={{0,1},{1,0},{2,3},{3,2},{4,5},{5,4},{6,7},{7,6},{8,9},{9,8},{10,11... | collective-permute-start | bytes 1769480 | tf_op jit(solution)/shard_map/ppermute | solution.py:46
  161.7 41.9 %all-to-all-start.5 = ((bf16[32,24,1664]{2,1,0:T(8,128)(2,1)}), bf16[32,24,1664]{2,1,0:T(8,128)(2,1)}, u32[]{:S(2)}, u32[]{:S(2)}) async-start(bf16[32,24,1664]{2,1,0:T(8,128)(2,1)} %bitcast.30), calls=%async_computation.5 | async-start | bytes 5111808 | tf_op jit(solution)/shard_map/all_to_all | solution.py:588
  168.3 44.7 %collective-permute-start.14 = (bf16[512,896]{1,0:T(8,128)(2,1)}, bf16[512,896]{1,0:T(8,128)(2,1)}, u32[]{:S(2)}, u32[]{:S(2)}) collective-permute-start(bf16[512,896]{1,0:T(8,128)(2,1)} %bitcast.34), channel_id=1, source_target_pairs={{0,64},{32,96},{64,0},{96,32},{1,65},{33,97},{65,1},{97,33},{2,66}... | collective-permute-start | bytes 2752520 | tf_op jit(solution)/shard_map/ppermute | solution.py:591
  176.1 16.1 %collective-permute-start.9 = (f32[256,768]{1,0:T(8,128)S(1)}, f32[256,768]{1,0:T(8,128)}, u32[]{:S(2)}, u32[]{:S(2)}) collective-permute-start(f32[256,768]{1,0:T(8,128)S(1)} %get-tuple-element.70.refs_4_.refs_8_), channel_id=1, source_target_pairs={{0,1},{1,0},{2,3},{3,2},{4,5},{5,4},{6,7},{7,6},{8,9},{9,8},{10,11... | collective-permute-start | bytes 2359304 | tf_op jit(solution)/shard_map/ppermute | solution.py:46
  176.1 36.9 %collective-permute-start.15 = (bf16[512,768]{1,0:T(8,128)(2,1)}, bf16[512,768]{1,0:T(8,128)(2,1)}, u32[]{:S(2)}, u32[]{:S(2)}) collective-permute-start(bf16[512,768]{1,0:T(8,128)(2,1)} %bitcast.9.refs_9_.refs_1_.refs_3_), channel_id=1, source_target_pairs={{0,64},{32,96},{64,0},{96,32},{1,65},{33,97},{65,1},{97,33},{2,66}... | collective-permute-start | bytes 2359304 | tf_op jit(solution)/shard_map/ppermute | solution.py:591
  178.1 14.0 %copy-start.8 = (f32[256,768]{1,0:T(8,128)S(1)}, f32[256,768]{1,0:T(8,128)}, u32[]{:S(2)}) copy-start(f32[256,768]{1,0:T(8,128)} %get-tuple-element.71.refs_1_) | copy-start | bytes 2359300
  178.1 14.0 %copy-start.13 = (bf16[256,768]{1,0:T(8,128)(2,1)S(1)}, bf16[256,768]{1,0:T(8,128)(2,1)}, u32[]{:S(2)}) copy-start(bf16[256,768]{1,0:T(8,128)(2,1)} %refs_0_.4) | copy-start | bytes 1179652
  206.8 14.4 %collective-permute-start.11 = (bf16[24,3328]{1,0:T(8,128)(2,1)S(1)}, bf16[24,3328]{1,0:T(8,128)(2,1)S(1)}, u32[]{:S(2)}, u32[]{:S(2)}) collective-permute-start(bf16[24,3328]{1,0:T(8,128)(2,1)S(1)} %shard_map.243.refs_6_.refs_0_), channel_id=1, source_target_pairs={{0,32},{32,64},{64,96},{96,0},{1,33},{33,65},{65,97},{97,1},{2,34}... | collective-permute-start | bytes 479240 | tf_op jit(solution)/shard_map/ppermute | solution.py:791
  208.7 12.4 %collective-permute-start.12 = (bf16[24,3328]{1,0:T(8,128)(2,1)S(1)}, bf16[24,3328]{1,0:T(8,128)(2,1)S(1)}, u32[]{:S(2)}, u32[]{:S(2)}) collective-permute-start(bf16[24,3328]{1,0:T(8,128)(2,1)S(1)} %shard_map.243.refs_6_.refs_0_), channel_id=1, source_target_pairs={{0,64},{32,96},{64,0},{96,32},{1,65},{33,97},{65,1},{97,33},{2,66}... | collective-permute-start | bytes 479240 | tf_op jit(solution)/shard_map/ppermute | solution.py:791
  211.6 9.5 %collective-permute-start.13 = (bf16[24,3328]{1,0:T(8,128)(2,1)S(1)}, bf16[24,3328]{1,0:T(8,128)(2,1)S(1)}, u32[]{:S(2)}, u32[]{:S(2)}) collective-permute-start(bf16[24,3328]{1,0:T(8,128)(2,1)S(1)} %shard_map.243.refs_6_.refs_0_), channel_id=1, source_target_pairs={{0,96},{32,0},{64,32},{96,64},{1,97},{33,1},{65,33},{97,65},{2,98}... | collective-permute-start | bytes 479240 | tf_op jit(solution)/shard_map/ppermute | solution.py:791
  (18 other events, 93.3 us)
